TPU v7x, 32 devices: a whole 2x2x4 slice. The times are simulated.
32 devices in a mesh: member: 2 (over y), space: 8 (over z, x), tracer: 2 (over core).
Axes of the slice: x: 2, y: 2, z: 4, core: 2. Of those that a mesh axis runs over, the one named last changes fastest.
Arguments:
- lam_new: float32 [48, 4, 64, 512], P(('member', 'tracer'), None, 'space'), parts along dimension 0, may hold values from -6 to 6
- tracers: float32 [48, 4, 64, 512], P(('member', 'tracer'), None, 'space'), parts along dimension 0, may hold values from -6 to 6
- velocity_u: float32 [8, 64, 512], P('member', 'space'), parts along dimension 0, may hold values from -3 to 3
- velocity_v: float32 [8, 64, 512], P('member', 'space'), parts along dimension 0, may hold values from -3 to 3
- diffusivity: float32 [8, 64, 512], P('member', 'space'), parts along dimension 0, may hold values from 0.05 to 0.3
- light: float32 [8, 64, 512], P('member', 'space'), parts along dimension 0, may hold values from 0.25 to 2
- land_sea: int32 [4, 64, 512], P(None, 'space'), may hold values 0 or 1
- partner: int32 [64], P('space'), may hold values from 0 to 63, as said below
- decay: float32 [24], P('tracer'), may hold values from 0.05 to 0.5
- w_in: float32 [8, 24], replicated, may hold values from -1.25 to 1.25
- w_out: float32 [24, 8], replicated, may hold values from -2 to 2
Outputs:
- lam_old: float32 [48, 4, 64, 512], P(('member', 'tracer'), None, 'space'), parts along dimension 0
There are 2 independent parts, one for each index of `member`. A program takes and returns all parts, laid end to end along the dimension named above; an argument that names none is the same for every part. Nothing has to cross between parts.
Inputs may be any that keep to these rules, and one draw needn't show every extreme that they name: partner[partner[i]] == i, and partner[i] lies in the mirrored block of 8 columns: partner[i] // 8 == 7 - i // 8.
All inputs are finite; a program needn't handle non-finite values. No bound on the sum of `land_sea` on one device may be relied on, other than what follows from the above.
Results may differ from a plain program's by a relative error of at most 0.00013.
Values sent between devices are 32-bit elements; how exact they have to be, the bound alone decides.
No kernel may reach another device: no remote copies, remote signals or barrier semaphores. Data moves between devices by JAX's collectives and lax.ppermute only.
A program may use at most 128 MiB of HBM per device.

v0:
```python
import functools

import jax
import jax.numpy as jnp
from jax import lax
from jax.experimental import pallas as pl
from jax.experimental.pallas import tpu as pltpu
from jax.sharding import PartitionSpec as P

F32 = jnp.float32
VMEM = pl.BlockSpec(memory_space=pltpu.VMEM)
SMEM = pl.BlockSpec(memory_space=pltpu.SMEM)


def sums_kernel(w_in, w_out, lam, tracers, vel_u, vel_v, kappa, sea_int, sums, pack_even, pack_odd):
    count, levels, cols, rows = lam.shape
    reactions = w_in.shape[0]
    first = lax.axis_index("tracer") * count
    even = lax.rem(lax.axis_index("space"), 2) == 0
    edge = count * levels

    for target, is_east in ((pack_even, even), (pack_odd, jnp.logical_not(even))):
        line = pl.ds(jnp.where(is_east, cols - 1, 0), 1)
        sign = jnp.where(is_east, -0.5, 0.5)
        for a in range(count):
            for k in range(levels):
                target[pl.ds(a * levels + k, 1), :] = lam[a, k, line, :]
        for k in range(levels):
            target[pl.ds(edge + k, 1), :] = 0.25 * vel_u[k, line, :] + sign * kappa[k, line, :]
            target[pl.ds(edge + levels + k, 1), :] = sea_int[k, line, :].astype(F32)

    lane = lax.broadcasted_iota(jnp.int32, (cols, 128), 1)
    top = jnp.zeros((cols, 128), F32)
    last = rows - 128
    for a in range(count):
        for k in range(levels):
            top = jnp.where(lane == a * levels + k, lam[a, k, :, last:][:, 127:], top)
    for k in range(levels):
        coef = 0.5 * kappa[k, :, last:] - 0.25 * vel_v[k, :, last:]
        top = jnp.where(lane == edge + k, coef[:, 127:], top)
        top = jnp.where(lane == edge + levels + k, sea_int[k, :, last:].astype(F32)[:, 127:], top)
    pack_odd[pl.ds(edge + 2 * levels, cols), :128] = top

    def level(k, carry):
        for field, weight, base in ((tracers, lambda h, a: w_in[h, first + a], 0), (lam, lambda h, a: w_out[h, first + a], reactions)):
            total = [None] * reactions
            for a in range(count):
                x = field[a, k]
                for h in range(reactions):
                    term = weight(h, a) * x
                    total[h] = term if a == 0 else total[h] + term
            for h in range(reactions):
                sums[base + h, k] = total[h]
        return carry

    lax.fori_loop(0, levels, level, 0)


def final_kernel(w_in, decay, partner, lam, vel_u, vel_v, kappa, light, sea_int, sums, sums_other, from_even, from_odd, from_fold, out, fold_rows, halo_e, halo_w):
    count, levels, cols, rows = lam.shape
    reactions = w_in.shape[0]
    first = lax.axis_index("tracer") * count
    place, strips = lax.axis_index("space"), lax.axis_size("space")
    even = lax.rem(place, 2) == 0
    edge = count * levels
    at = edge + 2 * levels
    neighbour = jnp.where(even, lax.rem(place + strips - 1, strips), lax.rem(place + 1, strips))
    folded = neighbour == strips - 1 - place
    fold = jnp.where(folded, from_odd[pl.ds(at, cols), :128], from_fold[...])
    halo_e[...] = jnp.where(even, from_even[...], from_odd[pl.ds(0, at), :])
    halo_w[...] = jnp.where(even, from_odd[pl.ds(0, at), :], from_even[...])
    sub = lax.broadcasted_iota(jnp.int32, (cols, 128), 0)
    turned = jnp.zeros((cols, 128), F32)
    for i in range(cols):
        pick = lax.rem(partner[i], cols)
        row = jnp.sum(jnp.where(sub == pick, fold, 0.0), axis=0, keepdims=True)
        turned = jnp.where(sub == i, row, turned)
    fold_rows[...] = turned

    col = lax.broadcasted_iota(jnp.int32, (cols, rows), 0)
    row = lax.broadcasted_iota(jnp.int32, (cols, rows), 1)
    is_east, is_west = col == cols - 1, col == 0
    is_top, is_bottom = row == rows - 1, row == 0
    lane = lax.broadcasted_iota(jnp.int32, (cols, 128), 1)

    def halo(ref, index):
        return ref[pl.ds(index, 1), :]

    def folded_at(index):
        return jnp.sum(jnp.where(lane == index, fold_rows[...], 0.0), axis=1, keepdims=True)

    def level(k, carry):
        sea = sea_int[k].astype(F32)
        u, v, kap = vel_u[k], vel_v[k], kappa[k]
        p, q = 0.25 * u + 0.5 * kap, 0.25 * u - 0.5 * kap
        pn, qn = 0.25 * v + 0.5 * kap, 0.25 * v - 0.5 * kap

        def eastern(x, index):
            return jnp.where(is_east, halo(halo_e, index), pltpu.roll(x, cols - 1, 0))

        def western(x, index):
            return jnp.where(is_west, halo(halo_w, index), pltpu.roll(x, 1, 0))

        def northern(x, index):
            return jnp.where(is_top, folded_at(index), pltpu.roll(x, rows - 1, 1))

        c_e = sea * eastern(sea, edge + levels + k) * (p + eastern(p, edge + k))
        c_w = sea * western(sea, edge + levels + k) * (western(q, edge + k) + q)
        c_n = sea * northern(sea, edge + levels + k) * (pn + northern(pn, edge + k))
        c_s = jnp.where(is_bottom, 0.0, sea * pltpu.roll(sea, 1, 1) * (pltpu.roll(qn, 1, 1) + qn))
        own = sea + (c_w + c_s - c_e - c_n)
        lit = light[k] * sea
        gain = []
        for h in range(reactions):
            t = jnp.tanh(sums[h, k] + sums_other[h, k])
            gain.append(lit * (1.0 - t * t) * (sums[reactions + h, k] + sums_other[reactions + h, k]))
        for a in range(count):
            x = lam[a, k]
            y = (own - decay[a] * sea) * x
            y += c_e * eastern(x, a * levels + k)
            y -= c_w * western(x, a * levels + k)
            y += c_n * northern(x, a * levels + k)
            y -= c_s * pltpu.roll(x, 1, 1)
            for h in range(reactions):
                y += w_in[h, first + a] * gain[h]
            out[a, k] = y
        return carry

    lax.fori_loop(0, levels, level, 0)


def body(lam, tracers, vel_u, vel_v, kappa, light, sea_int, partner, decay, w_in, w_out):
    count, levels, cols, rows = lam.shape
    reactions = w_in.shape[0]
    edge = (count + 2) * levels
    n = lax.axis_size("space")
    sums, pack_even, pack_odd = pl.pallas_call(
        sums_kernel,
        name="sums",
        out_shape=(
            jax.ShapeDtypeStruct((2 * reactions, levels, cols, rows), F32),
            jax.ShapeDtypeStruct((edge, rows), F32),
            jax.ShapeDtypeStruct((edge + cols, rows), F32),
        ),
        in_specs=[SMEM, SMEM] + [VMEM] * 6,
        out_specs=(VMEM, VMEM, VMEM),
        compiler_params=pltpu.CompilerParams(vmem_limit_bytes=32 << 20),
    )(w_in, w_out.T, lam, tracers, vel_u, vel_v, kappa, sea_int)
    even_pairs = [(s, s ^ 1) for s in range(n)]
    odd_pairs = [(s, (s + 1) % n if s % 2 else (s - 1) % n) for s in range(n)]
    fold_pairs = [(s, n - 1 - s) for s in range(n) if (s, n - 1 - s) not in odd_pairs]
    top = pack_odd[edge:, :128]
    sums_other = lax.ppermute(sums, "tracer", [(0, 1), (1, 0)])
    from_odd = lax.ppermute(pack_odd, "space", odd_pairs)
    from_even = lax.ppermute(pack_even, "space", even_pairs)
    from_fold = lax.ppermute(top, "space", fold_pairs)
    return pl.pallas_call(
        final_kernel,
        name="final",
        out_shape=jax.ShapeDtypeStruct(lam.shape, F32),
        in_specs=[SMEM] * 3 + [VMEM] * 11,
        out_specs=VMEM,
        scratch_shapes=[
            pltpu.VMEM((cols, 128), F32),
            pltpu.VMEM((edge, rows), F32),
            pltpu.VMEM((edge, rows), F32),
        ],
        compiler_params=pltpu.CompilerParams(vmem_limit_bytes=32 << 20),
    )(w_in, decay, partner, lam, vel_u, vel_v, kappa, light, sea_int, sums, sums_other, from_even, from_odd, from_fold)


def solution(mesh):
    placed = (
        P(("member", "tracer"), None, "space", None),
        P(("member", "tracer"), None, "space", None),
        P("member", "space", None),
        P("member", "space", None),
        P("member", "space", None),
        P("member", "space", None),
        P(None, "space", None),
        P("space"),
        P("tracer"),
        P(),
        P(),
    )
    return jax.shard_map(
        body,
        mesh=mesh,
        in_specs=placed,
        out_specs=P(("member", "tracer"), None, "space", None),
        check_vma=False,
    )
```

profile of v0, /device:TPU:2, one launch (start us, length us, event | category | flops | bytes accessed | tf_op | source)
XLA Modules:
  0.0 25.5 jit_solution(8453777028348653219)
XLA Ops:
  0.0 0.0 copy-start
  0.0 1.1 %copy-done = f32[12,4,8,512]{3,2,1,0:T(8,128)S(1)} copy-done((f32[12,4,8,512]{3,2,1,0:T(8,128)S(1)}, f32[12,4,8,512]{3,2,1,0:T(8,128)}, u32[]{:S(2)}) %copy-start) | copy-done | bytes 786456
  1.1 0.0 copy-start.2
  1.1 1.1 %copy-done.2 = f32[12,4,8,512]{3,2,1,0:T(8,128)S(1)} copy-done((f32[12,4,8,512]{3,2,1,0:T(8,128)S(1)}, f32[12,4,8,512]{3,2,1,0:T(8,128)}, u32[]{:S(2)}) %copy-start.2) | copy-done | bytes 786456
  2.3 0.0 copy-start.3
  2.3 0.8 %copy-done.3 = f32[4,8,512]{2,1,0:T(8,128)S(1)} copy-done((f32[4,8,512]{2,1,0:T(8,128)S(1)}, f32[4,8,512]{2,1,0:T(8,128)}, u32[]{:S(2)}) %copy-start.3) | copy-done | bytes 65560
  3.1 0.0 copy-start.5
  3.1 0.8 %copy-done.5 = f32[4,8,512]{2,1,0:T(8,128)S(1)} copy-done((f32[4,8,512]{2,1,0:T(8,128)S(1)}, f32[4,8,512]{2,1,0:T(8,128)}, u32[]{:S(2)}) %copy-start.5) | copy-done | bytes 65560
  3.9 0.0 copy-start.7
  4.0 0.8 %copy-done.7 = f32[4,8,512]{2,1,0:T(8,128)S(1)} copy-done((f32[4,8,512]{2,1,0:T(8,128)S(1)}, f32[4,8,512]{2,1,0:T(8,128)}, u32[]{:S(2)}) %copy-start.7) | copy-done | bytes 65560
  4.8 0.0 copy-start.9
  4.8 0.8 %copy-done.9 = s32[4,8,512]{2,1,0:T(8,128)S(1)} copy-done((s32[4,8,512]{2,1,0:T(8,128)S(1)}, s32[4,8,512]{2,1,0:T(8,128)}, u32[]{:S(2)}) %copy-start.9) | copy-done | bytes 65560
  5.6 0.0 copy-start.12
  5.6 0.7 %copy-done.12 = f32[8,24]{1,0:T(8,128)S(1)} copy-done((f32[8,24]{1,0:T(8,128)S(1)}, f32[8,24]{1,0:T(8,128)}, u32[]{:S(2)}) %copy-start.12) | copy-done | bytes 792
  6.3 0.0 copy-start.13
  6.3 0.7 %copy-done.13 = f32[24,8]{0,1:T(8,128)S(1)} copy-done((f32[24,8]{0,1:T(8,128)S(1)}, f32[24,8]{0,1:T(8,128)}, u32[]{:S(2)}) %copy-start.13) | copy-done | bytes 792
  7.0 0.0 copy-start.1
  7.0 0.0 copy-start.4
  7.0 0.0 copy-start.6
  7.0 0.0 copy-start.8
  7.0 0.0 copy-start.10
  7.0 0.0 copy-start.11
  7.0 1.9 %sums.1 = (f32[16,4,8,512]{3,2,1,0:T(8,128)S(1)}, f32[56,512]{1,0:T(8,128)S(1)}, f32[64,512]{1,0:T(8,128)S(1)}) custom-call(f32[8,24]{1,0:T(8,128)S(1)} %copy-done.12, f32[8,24]{1,0:T(8,128)S(1)} %bitcast.1, f32[12,4,8,512]{3,2,1,0:T(8,128)S(1)} %copy-done, f32[12,4,8,512]{3,2,1,0:T(8,128)S(1)} %copy-done.2, f32[4,8,512]{2,1,0:T(8,128)S(1)} %copy-done.3, ...), custom_call_target="tpu_custom_call" | custom-call | tf_op jit(solution)/shard_map/sums/pallas_call | solution.py:137
  8.9 0.1 collective-permute-start
  9.0 1.6 %collective-permute-start.2 = (f32[64,512]{1,0:T(8,128)S(1)}, f32[64,512]{1,0:T(8,128)S(1)}, u32[]{:S(2)}, u32[]{:S(2)}) collective-permute-start(f32[64,512]{1,0:T(8,128)S(1)} %get-tuple-element.10), channel_id=1, source_target_pairs={{0,14},{2,4},{4,2},{6,8},{8,6},{10,12},{12,10},{14,0},{1,15},{3,5}... | collective-permute-start | bytes 393224 | tf_op jit(solution)/shard_map/ppermute | solution.py:154
  10.6 0.0 copy-start.14
  10.6 0.0 copy-start.15
  10.6 3.5 %collective-permute-start.1 = (f32[56,512]{1,0:T(8,128)S(1)}, f32[56,512]{1,0:T(8,128)S(1)}, u32[]{:S(2)}, u32[]{:S(2)}) collective-permute-start(f32[56,512]{1,0:T(8,128)S(1)} %get-tuple-element.9), channel_id=1, source_target_pairs={{0,2},{2,0},{4,6},{6,4},{8,10},{10,8},{12,14},{14,12},{1,3},{3,1},... | collective-permute-start | bytes 344072 | tf_op jit(solution)/shard_map/ppermute | solution.py:155
  14.1 2.0 %collective-permute-start.3 = (f32[8,128]{1,0:T(8,128)S(1)}, f32[8,128]{1,0:T(8,128)S(1)}, u32[]{:S(2)}, u32[]{:S(2)}) collective-permute-start(f32[8,128]{1,0:T(8,128)S(1)} %slice.3), channel_id=1, source_target_pairs={{2,12},{4,10},{10,4},{12,2},{3,13},{5,11},{11,5},{13,3},{18,28},{2... | collective-permute-start | bytes 12296 | tf_op jit(solution)/shard_map/ppermute | solution.py:156
  16.1 6.2 %collective-permute-done.3.from_fold = f32[8,128]{1,0:T(8,128)S(1)} collective-permute-done((f32[8,128]{1,0:T(8,128)S(1)}, f32[8,128]{1,0:T(8,128)S(1)}, u32[]{:S(2)}, u32[]{:S(2)}) %collective-permute-start.3) | collective-permute-done | bytes 4128 | tf_op jit(solution)/shard_map/ppermute | solution.py:156
  22.3 0.0 collective-permute-done.1.from_even
  22.3 0.0 collective-permute-done.2.from_odd
  22.3 0.0 collective-permute-done.sums_other
  22.3 0.0 copy-done.1
  22.3 0.0 copy-done.4
  22.3 0.0 copy-done.6
  22.3 0.0 copy-done.8
  22.4 0.0 copy-done.10
  22.4 0.0 copy-done.11
  22.4 0.0 copy-done.14
  22.4 0.0 copy-done.15
  22.4 3.1 %final.1 = f32[12,4,8,512]{3,2,1,0:T(8,128)} custom-call(f32[8,24]{1,0:T(8,128)S(1)} %copy-done.12, f32[12]{0:T(128)S(1)} %copy-done.14, s32[8]{0:T(128)S(1)} %copy-done.15, f32[12,4,8,512]{3,2,1,0:T(8,128)S(1)} %copy-done.1, f32[4,8,512]{2,1,0:T(8,128)S(1)} %copy-done.4, f32[4,8,512]{2,1,0:T(8,128)S(1)} %copy-done.6, f32[4,8,512]{2,1,0:T(8,128)S(1)} %copy-done.8, ...), custom_call_target="tpu_custom_call" | custom-call | tf_op jit(solution)/shard_map/final/pallas_call | solution.py:157
  (1 shorter events, 0.0 us)
Async XLA Ops:
  0.0 1.1 %copy-start = (f32[12,4,8,512]{3,2,1,0:T(8,128)S(1)}, f32[12,4,8,512]{3,2,1,0:T(8,128)}, u32[]{:S(2)}) copy-start(f32[12,4,8,512]{3,2,1,0:T(8,128)} %lam.3) | copy-start | bytes 2359300
  1.1 1.1 %copy-start.2 = (f32[12,4,8,512]{3,2,1,0:T(8,128)S(1)}, f32[12,4,8,512]{3,2,1,0:T(8,128)}, u32[]{:S(2)}) copy-start(f32[12,4,8,512]{3,2,1,0:T(8,128)} %tracers.1) | copy-start | bytes 2359300
  2.3 0.8 %copy-start.3 = (f32[4,8,512]{2,1,0:T(8,128)S(1)}, f32[4,8,512]{2,1,0:T(8,128)}, u32[]{:S(2)}) copy-start(f32[4,8,512]{2,1,0:T(8,128)} %vel_u.3) | copy-start | bytes 196612
  3.1 0.8 %copy-start.5 = (f32[4,8,512]{2,1,0:T(8,128)S(1)}, f32[4,8,512]{2,1,0:T(8,128)}, u32[]{:S(2)}) copy-start(f32[4,8,512]{2,1,0:T(8,128)} %vel_v.3) | copy-start | bytes 196612
  3.9 0.8 %copy-start.7 = (f32[4,8,512]{2,1,0:T(8,128)S(1)}, f32[4,8,512]{2,1,0:T(8,128)}, u32[]{:S(2)}) copy-start(f32[4,8,512]{2,1,0:T(8,128)} %kappa.3) | copy-start | bytes 196612
  4.8 0.8 %copy-start.9 = (s32[4,8,512]{2,1,0:T(8,128)S(1)}, s32[4,8,512]{2,1,0:T(8,128)}, u32[]{:S(2)}) copy-start(s32[4,8,512]{2,1,0:T(8,128)} %sea_int.3) | copy-start | bytes 196612
  5.6 0.7 %copy-start.12 = (f32[8,24]{1,0:T(8,128)S(1)}, f32[8,24]{1,0:T(8,128)}, u32[]{:S(2)}) copy-start(f32[8,24]{1,0:T(8,128)} %w_in.3) | copy-start | bytes 2308
  6.3 0.7 %copy-start.13 = (f32[24,8]{0,1:T(8,128)S(1)}, f32[24,8]{0,1:T(8,128)}, u32[]{:S(2)}) copy-start(f32[24,8]{0,1:T(8,128)} %param.21) | copy-start | bytes 2308
  7.0 15.3 %copy-start.1 = (f32[12,4,8,512]{3,2,1,0:T(8,128)S(1)}, f32[12,4,8,512]{3,2,1,0:T(8,128)}, u32[]{:S(2)}) copy-start(f32[12,4,8,512]{3,2,1,0:T(8,128)} %lam.3) | copy-start | bytes 2359300
  7.0 15.3 %copy-start.4 = (f32[4,8,512]{2,1,0:T(8,128)S(1)}, f32[4,8,512]{2,1,0:T(8,128)}, u32[]{:S(2)}) copy-start(f32[4,8,512]{2,1,0:T(8,128)} %vel_u.3) | copy-start | bytes 196612
  7.0 15.3 %copy-start.6 = (f32[4,8,512]{2,1,0:T(8,128)S(1)}, f32[4,8,512]{2,1,0:T(8,128)}, u32[]{:S(2)}) copy-start(f32[4,8,512]{2,1,0:T(8,128)} %vel_v.3) | copy-start | bytes 196612
  7.0 15.3 %copy-start.8 = (f32[4,8,512]{2,1,0:T(8,128)S(1)}, f32[4,8,512]{2,1,0:T(8,128)}, u32[]{:S(2)}) copy-start(f32[4,8,512]{2,1,0:T(8,128)} %kappa.3) | copy-start | bytes 196612
  7.0 15.3 %copy-start.10 = (s32[4,8,512]{2,1,0:T(8,128)S(1)}, s32[4,8,512]{2,1,0:T(8,128)}, u32[]{:S(2)}) copy-start(s32[4,8,512]{2,1,0:T(8,128)} %sea_int.3) | copy-start | bytes 196612
  7.0 15.3 %copy-start.11 = (f32[4,8,512]{2,1,0:T(8,128)S(1)}, f32[4,8,512]{2,1,0:T(8,128)}, u32[]{:S(2)}) copy-start(f32[4,8,512]{2,1,0:T(8,128)} %light.1) | copy-start | bytes 196612
  8.9 13.4 %collective-permute-start = (f32[16,4,8,512]{3,2,1,0:T(8,128)S(1)}, f32[16,4,8,512]{3,2,1,0:T(8,128)S(1)}, u32[]{:S(2)}, u32[]{:S(2)}) collective-permute-start(f32[16,4,8,512]{3,2,1,0:T(8,128)S(1)} %get-tuple-element.8.sums), channel_id=1, source_target_pairs={{0,1},{1,0},{2,3},{3,2},{4,5},{5,4},{6,7},{7,6},{8,9},{9,8},{10,11... | collective-permute-start | bytes 3145736 | tf_op jit(solution)/shard_map/ppermute | solution.py:153
  9.0 13.3 %collective-permute-start.2 = (f32[64,512]{1,0:T(8,128)S(1)}, f32[64,512]{1,0:T(8,128)S(1)}, u32[]{:S(2)}, u32[]{:S(2)}) collective-permute-start(f32[64,512]{1,0:T(8,128)S(1)} %get-tuple-element.10), channel_id=1, source_target_pairs={{0,14},{2,4},{4,2},{6,8},{8,6},{10,12},{12,10},{14,0},{1,15},{3,5}... | collective-permute-start | bytes 393224 | tf_op jit(solution)/shard_map/ppermute | solution.py:154
  10.6 11.8 %copy-start.14 = (f32[12]{0:T(128)S(1)}, f32[12]{0:T(128)}, u32[]{:S(2)}) copy-start(f32[12]{0:T(128)} %decay.1) | copy-start | bytes 148
  10.6 11.8 %copy-start.15 = (s32[8]{0:T(128)S(1)}, s32[8]{0:T(128)}, u32[]{:S(2)}) copy-start(s32[8]{0:T(128)} %partner.1) | copy-start | bytes 100
  10.6 11.7 %collective-permute-start.1 = (f32[56,512]{1,0:T(8,128)S(1)}, f32[56,512]{1,0:T(8,128)S(1)}, u32[]{:S(2)}, u32[]{:S(2)}) collective-permute-start(f32[56,512]{1,0:T(8,128)S(1)} %get-tuple-element.9), channel_id=1, source_target_pairs={{0,2},{2,0},{4,6},{6,4},{8,10},{10,8},{12,14},{14,12},{1,3},{3,1},... | collective-permute-start | bytes 344072 | tf_op jit(solution)/shard_map/ppermute | solution.py:155
  14.1 8.2 %collective-permute-start.3 = (f32[8,128]{1,0:T(8,128)S(1)}, f32[8,128]{1,0:T(8,128)S(1)}, u32[]{:S(2)}, u32[]{:S(2)}) collective-permute-start(f32[8,128]{1,0:T(8,128)S(1)} %slice.3), channel_id=1, source_target_pairs={{2,12},{4,10},{10,4},{12,2},{3,13},{5,11},{11,5},{13,3},{18,28},{2... | collective-permute-start | bytes 12296 | tf_op jit(solution)/shard_map/ppermute | solution.py:156
where the time goes:
time: 26 us; the launch traced here: 25.5 us
  starting transfers between devices  7.2 us (28%)
  local copies, waits for them, and re-layouts  7.03 us (27%)
  waiting for transfers between devices  6.19 us (24%)
  Pallas kernels  4.99 us (19%)
    unnamed x32, local copies, waits for them, and re-layouts  7.02 us
    ppermute x1, waiting for transfers between devices, body(): from_fold = lax.ppermute(top, 'space', fold_pairs)  6.18 us
    ppermute x1, starting transfers between devices, body(): from_even = lax.ppermute(pack_even, 'space', even_pairs)  3.52 us
    pallas_call x1, Pallas kernels, body(): pl.pallas_call(final_kernel, name='final', out_shape=jax.ShapeDtypeStruct...  3.13 us
    ppermute x1, starting transfers between devices, body(): from_fold = lax.ppermute(top, 'space', fold_pairs)  2 us
    pallas_call x1, Pallas kernels, body(): pl.pallas_call(sums_kernel, name='sums', out_shape=(jax.ShapeDtypeStruct(...  1.86 us
    ppermute x1, starting transfers between devices, body(): from_odd = lax.ppermute(pack_odd, 'space', odd_pairs)  1.61 us
  transfers between devices with their start and end apart: 4, of which 1 were waited for; matrix products, arithmetic and copies ran while one was open for 0% of the time, Pallas kernels for 0%

commit v1 on v0

v1 whole, which is shorter than its diff:
```python
import jax
import jax.numpy as jnp
from jax import lax
from jax.experimental import pallas as pl
from jax.experimental.pallas import tpu as pltpu
from jax.sharding import PartitionSpec as P

F32 = jnp.float32
VMEM = pl.BlockSpec(memory_space=pltpu.VMEM)
SMEM = pl.BlockSpec(memory_space=pltpu.SMEM)
HBM = pl.BlockSpec(memory_space=pltpu.HBM)
LANES = 128


def pack_kernel(
    vel_u_hbm, vel_v_hbm, kappa_hbm, sea_hbm, lam_hbm, tracers_hbm, light_hbm, w_in_hbm, w_out_hbm, decay_hbm, partner_hbm,
    vel_u, vel_v, kappa, sea, lam, tracers, light, w_in, w_out, decay, partner, pack_east, pack_west, top_out, sems,
):
    count, levels, cols, rows = lam.shape
    edge = count * levels
    tall = edge + 2 * levels
    sources = (vel_u_hbm, vel_v_hbm, kappa_hbm, sea_hbm, lam_hbm, tracers_hbm, light_hbm, w_in_hbm, w_out_hbm, decay_hbm, partner_hbm)
    targets = (vel_u, vel_v, kappa, sea, lam, tracers, light, w_in, w_out, decay, partner)
    copies = [pltpu.make_async_copy(s, t, sems.at[i]) for i, (s, t) in enumerate(zip(sources, targets))]
    for copy in copies:
        copy.start()
    for copy in copies[:5]:
        copy.wait()

    for target, line, sign in ((pack_east, slice(cols - 1, cols), -0.5), (pack_west, slice(0, 1), 0.5)):

        def put(index, value):
            for c in range(rows // LANES):
                target[pl.ds(c * tall + index, 1), :] = value[:, c * LANES : (c + 1) * LANES]

        for a in range(count):
            for k in range(levels):
                put(a * levels + k, lam[a, k, line, :])
        for k in range(levels):
            put(edge + k, 0.25 * vel_u[k, line, :] + sign * kappa[k, line, :])
            put(edge + levels + k, sea[k, line, :].astype(F32))

    lane = lax.broadcasted_iota(jnp.int32, (cols, LANES), 1)
    top = jnp.zeros((cols, LANES), F32)
    last = rows - LANES

    def placed(top, index, value):
        return jnp.where(lane == index, pltpu.roll(value, index + 1, 1), top)

    for a in range(count):
        for k in range(levels):
            top = placed(top, a * levels + k, lam[a, k, :, last:])
    for k in range(levels):
        top = placed(top, edge + k, 0.5 * kappa[k, :, last:] - 0.25 * vel_v[k, :, last:])
        top = placed(top, edge + levels + k, sea[k, :, last:].astype(F32))
    for target in (pack_east, pack_west):
        target[pl.ds(rows // LANES * tall, cols), :] = top
    top_out[...] = top
    for copy in copies[5:]:
        copy.wait()


def sums_kernel(w_in, w_out, lam, tracers, sums):
    count, levels, cols, rows = lam.shape
    reactions = w_in.shape[0]
    first = lax.axis_index("tracer") * count

    def level(k, carry):
        for field, weight, base in ((tracers, w_in, 0), (lam, w_out, reactions)):
            total = [None] * reactions
            for a in range(count):
                x = field[a, k]
                for h in range(reactions):
                    term = weight[h, first + a] * x
                    total[h] = term if a == 0 else total[h] + term
            for h in range(reactions):
                sums[base + h, k] = total[h]
        return carry

    lax.fori_loop(0, levels, level, 0)


def inner_kernel(decay, lam, vel_u, vel_v, kappa, sea_int, out):
    count, levels, cols, rows = lam.shape
    col = lax.broadcasted_iota(jnp.int32, (cols, rows), 0)
    row = lax.broadcasted_iota(jnp.int32, (cols, rows), 1)

    def level(k, carry):
        sea = sea_int[k].astype(F32)
        u, v, kap = 0.25 * vel_u[k], 0.25 * vel_v[k], 0.5 * kappa[k]
        east = jnp.where(col == cols - 1, 0.0, sea * pltpu.roll(sea, cols - 1, 0))
        north = jnp.where(row == rows - 1, 0.0, sea * pltpu.roll(sea, rows - 1, 1))
        p, q = u + kap, u - kap
        pn, qn = v + kap, v - kap
        c_e = east * (p + pltpu.roll(p, cols - 1, 0))
        c_w = pltpu.roll(east * (q + pltpu.roll(q, cols - 1, 0)), 1, 0)
        c_n = north * (pn + pltpu.roll(pn, rows - 1, 1))
        c_s = pltpu.roll(north * (qn + pltpu.roll(qn, rows - 1, 1)), 1, 1)
        own = sea + (c_w + c_s - c_e - c_n)
        for a in range(count):
            x = lam[a, k]
            y = (own - decay[a] * sea) * x
            y += c_e * pltpu.roll(x, cols - 1, 0)
            y -= c_w * pltpu.roll(x, 1, 0)
            y += c_n * pltpu.roll(x, rows - 1, 1)
            y -= c_s * pltpu.roll(x, 1, 1)
            out[a, k] = y
        return carry

    lax.fori_loop(0, levels, level, 0)


def react_kernel(w_in, light, sea, sums, sums_other, inner, out):
    count, levels, cols, rows = inner.shape
    reactions = w_in.shape[0]
    first = lax.axis_index("tracer") * count

    def level(k, carry):
        lit = light[k] * sea[k].astype(F32)
        gain = []
        for h in range(reactions):
            t = jnp.tanh(sums[h, k] + sums_other[h, k])
            gain.append(lit * (1.0 - t * t) * (sums[reactions + h, k] + sums_other[reactions + h, k]))
        for a in range(count):
            y = inner[a, k]
            for h in range(reactions):
                y += w_in[h, first + a] * gain[h]
            out[a, k] = y
        return carry

    lax.fori_loop(0, levels, level, 0)


def edges_kernel(
    partner, lam, vel_u, vel_v, kappa, sea_int, inner, from_west, from_east, from_fold, out_hbm,
    out, turned, sems,
):
    count, levels, cols, rows = lam.shape
    edge = count * levels
    tall = edge + 2 * levels
    chunks = rows // LANES
    place, strips = lax.axis_index("space"), lax.axis_size("space")
    to_east, to_west = lax.rem(place + 1, strips), lax.rem(place + strips - 1, strips)
    mirror = strips - 1 - place
    for i in range(cols):
        pick = lax.rem(partner[i], cols)
        across = from_fold[pl.ds(pick, 1), :]
        across = jnp.where(mirror == to_east, from_east[pl.ds(chunks * tall + pick, 1), :], across)
        across = jnp.where(mirror == to_west, from_west[pl.ds(chunks * tall + pick, 1), :], across)
        turned[pl.ds(i, 1), :] = across
    sub = lax.broadcasted_iota(jnp.int32, (cols, LANES), 0)
    lane = lax.broadcasted_iota(jnp.int32, (cols, LANES), 1)
    side = jnp.where(sub == 0, -1.0, jnp.where(sub == cols - 1, 1.0, 0.0))
    across = turned[...]

    def beyond(c, index):
        at = pl.ds(c * tall + index, 1)
        return jnp.where(sub == 0, from_west[at, :], from_east[at, :])

    def folded_at(index):
        return pltpu.roll(across, LANES - 1 - index, 1)

    def copy(k):
        return pltpu.make_async_copy(out.at[:, k], out_hbm.at[:, k], sems.at[k])

    for k in range(levels):
        for c in range(chunks):
            part = slice(c * LANES, (c + 1) * LANES)
            sea, u, kap = sea_int[k, :, part].astype(F32), 0.25 * vel_u[k, :, part], 0.5 * kappa[k, :, part]
            mine = jnp.where(sub == 0, u - kap, u + kap)
            coef = side * sea * beyond(c, edge + levels + k) * (mine + beyond(c, edge + k))
            if c == chunks - 1:
                up = 0.25 * vel_v[k, :, part] + kap + folded_at(edge + k)
                fold = jnp.where(lane == LANES - 1, sea * folded_at(edge + levels + k) * up, 0.0)
            for a in range(count):
                x = lam[a, k, :, part]
                y = inner[a, k, :, part] + coef * (beyond(c, a * levels + k) - x)
                if c == chunks - 1:
                    y += fold * (folded_at(a * levels + k) - x)
                out[a, k, :, part] = y
        copy(k).start()
    for k in range(levels):
        copy(k).wait()


def cost(flops, count):
    return pl.CostEstimate(flops=0, bytes_accessed=0, transcendentals=0)


def body(lam, tracers, vel_u, vel_v, kappa, light, sea_int, partner, decay, w_in, w_out):
    count, levels, cols, rows = lam.shape
    reactions = w_in.shape[0]
    tall = (count + 2) * levels * (rows // LANES)
    n = lax.axis_size("space")
    params = pltpu.CompilerParams(vmem_limit_bytes=32 << 20)
    whole = jax.ShapeDtypeStruct(lam.shape, F32)
    shares = jax.ShapeDtypeStruct((2 * reactions, levels, cols, rows), F32)
    tile = jax.ShapeDtypeStruct((cols, LANES), F32)
    arguments = (vel_u, vel_v, kappa, sea_int, lam, tracers, light, w_in, w_out.T, decay, partner)
    vel_u, vel_v, kappa, sea_int, lam, tracers, light, w_in, w_out, decay, partner, pack_east, pack_west, top = pl.pallas_call(
        pack_kernel,
        name="pack",
        out_shape=(
            *(jax.ShapeDtypeStruct(x.shape, x.dtype) for x in arguments),
            jax.ShapeDtypeStruct((tall + cols, LANES), F32),
            jax.ShapeDtypeStruct((tall + cols, LANES), F32),
            tile,
        ),
        in_specs=[HBM] * 11,
        out_specs=(VMEM,) * 14,
        scratch_shapes=[pltpu.SemaphoreType.DMA((11,))],
        compiler_params=params,
        cost_estimate=cost(0, 4 * lam.size),
    )(*(pltpu.with_memory_space_constraint(x, pltpu.HBM) for x in arguments))
    eastward = [(s, (s + 1) % n) for s in range(n)]
    westward = [(s, (s - 1) % n) for s in range(n)]
    mirrored = [(s, n - 1 - s) for s in range(n)]
    from_fold = lax.ppermute(top, "space", [p for p in mirrored if p not in eastward + westward])
    from_east = lax.ppermute(pack_west, "space", westward)
    from_west = lax.ppermute(pack_east, "space", eastward)
    sums = pl.pallas_call(
        sums_kernel,
        name="sums",
        out_shape=shares,
        in_specs=[SMEM] * 2 + [VMEM] * 2,
        out_specs=VMEM,
        compiler_params=params,
        cost_estimate=cost(32 * lam.size, 4 * lam.size),
    )(w_in, w_out, lam, tracers)
    sums_other = lax.ppermute(sums, "tracer", [(0, 1), (1, 0)])
    inner = pl.pallas_call(
        inner_kernel,
        name="inner",
        out_shape=whole,
        in_specs=[SMEM] + [VMEM] * 5,
        out_specs=VMEM,
        compiler_params=params,
        cost_estimate=cost(10 * lam.size, 4 * lam.size),
    )(decay, lam, vel_u, vel_v, kappa, sea_int)
    inner = pl.pallas_call(
        react_kernel,
        name="react",
        out_shape=whole,
        in_specs=[SMEM] + [VMEM] * 5,
        out_specs=VMEM,
        compiler_params=params,
        cost_estimate=cost(16 * lam.size, 4 * lam.size),
    )(w_in, light, sea_int, sums, sums_other, inner)
    return pl.pallas_call(
        edges_kernel,
        name="edges",
        out_shape=whole,
        in_specs=[SMEM] + [VMEM] * 9,
        out_specs=HBM,
        scratch_shapes=[
            pltpu.VMEM(lam.shape, F32),
            pltpu.VMEM((cols, LANES), F32),
            pltpu.SemaphoreType.DMA((levels,)),
        ],
        compiler_params=params,
        cost_estimate=cost(10 * lam.size, 4 * lam.size),
    )(partner, lam, vel_u, vel_v, kappa, sea_int, inner, from_west, from_east, from_fold)


def solution(mesh):
    placed = (
        P(("member", "tracer"), None, "space", None),
        P(("member", "tracer"), None, "space", None),
        P("member", "space", None),
        P("member", "space", None),
        P("member", "space", None),
        P("member", "space", None),
        P(None, "space", None),
        P("space"),
        P("tracer"),
        P(),
        P(),
    )
    return jax.shard_map(
        body,
        mesh=mesh,
        in_specs=placed,
        out_specs=P(("member", "tracer"), None, "space", None),
        check_vma=False,
    )
```

time: 26 us -> 16.5 us (0.63); the launches traced: 25.5 us -> 16.3 us
  local copies, waits for them, and re-layouts: 7.03 us -> 0 us
  waiting for transfers between devices: 6.19 us -> 0.01 us
  Pallas kernels: 4.99 us -> 7.71 us
  starting transfers between devices: 7.2 us -> 8.52 us
    unnamed x32 -> x0, local copies, waits for them, and re-layouts: 7.02 us -> none
    ppermute x3, waiting for transfers between devices: 6.19 us -> 0.01 us  [the longest x1 0.01 us: body(): lax.ppermute(top, 'space', [p for p in mirrored if p not in eastward + we...]
    pallas_call x2 -> x5, Pallas kernels: 4.99 us -> 7.71 us  [the longest x1 1.71 us: body(): pl.pallas_call(sums_kernel, name='sums', out_shape=shares, in_specs=[SMEM...]
    ppermute x3, starting transfers between devices: 7.12 us -> 8.45 us  [the longest x1 6.37 us: body(): lax.ppermute(top, 'space', [p for p in mirrored if p not in eastward + we...]
  transfers between devices with their start and end apart: 4 -> 4, of which waited for: 1 -> 0; matrix products, arithmetic and copies ran while one was open for 0% -> 0% of each run, Pallas kernels for 0% -> 17%
where the time goes in v1:
time: 16.5 us; the launch traced here: 16.3 us
  starting transfers between devices  8.52 us (52%)
  Pallas kernels  7.71 us (47%)
    ppermute x1, starting transfers between devices, body(): lax.ppermute(top, 'space', [p for p in mirrored if p not in eastward + we...  6.37 us
    pallas_call x1, Pallas kernels, body(): pl.pallas_call(sums_kernel, name='sums', out_shape=shares, in_specs=[SMEM...  1.71 us
    pallas_call x1, Pallas kernels, body(): pl.pallas_call(pack_kernel, name='pack', out_shape=(*(jax.ShapeDtypeStruc...  1.65 us
    ppermute x1, starting transfers between devices, body(): from_west = lax.ppermute(pack_east, 'space', eastward)  1.6 us
    pallas_call x1, Pallas kernels, body(): pl.pallas_call(edges_kernel, name='edges', out_shape=whole, in_specs=[SME...  1.59 us
    pallas_call x1, Pallas kernels, body(): pl.pallas_call(inner_kernel, name='inner', out_shape=whole, in_specs=[SME...  1.47 us
    pallas_call x1, Pallas kernels, body(): pl.pallas_call(react_kernel, name='react', out_shape=whole, in_specs=[SME...  1.28 us
    ppermute x1, starting transfers between devices, body(): from_east = lax.ppermute(pack_west, 'space', westward)  0.48 us
  transfers between devices with their start and end apart: 4, of which 0 were waited for; matrix products, arithmetic and copies ran while one was open for 0% of the time, Pallas kernels for 17%

profile of v1, /device:TPU:2, one launch (start us, length us, event | category | flops | bytes accessed | tf_op | source)
XLA Modules:
  0.0 16.3 jit_solution(5232506616474886235)
XLA Ops:
  0.0 1.6 %pack.1 = (f32[4,8,512]{2,1,0:T(8,128)S(1)}, f32[4,8,512]{2,1,0:T(8,128)S(1)}, f32[4,8,512]{2,1,0:T(8,128)S(1)}, s32[4,8,512]{2,1,0:T(8,128)S(1)}, f32[12,4,8,51...) custom-call(f32[4,8,512]{2,1,0:T(8,128)} %vel_u_hbm.1, ...), custom_call_target="tpu_custom_call" | custom-call | tf_op jit(solution)/shard_map/pack/pallas_call | solution.py:200
  1.7 1.7 %sums.1 = f32[16,4,8,512]{3,2,1,0:T(8,128)S(1)} custom-call(f32[8,24]{1,0:T(8,128)S(1)} %get-tuple-element.25.w_in, f32[8,24]{1,0:T(8,128)S(1)} %get-tuple-element.27.w_out, f32[12,4,8,512]{3,2,1,0:T(8,128)S(1)} %get-tuple-element.20.lam, f32[12,4,8,512]{3,2,1,0:T(8,128)S(1)} %get-tuple-element.28.tracers), custom_call_target="tpu_custom_call" | custom-call | tf_op jit(solution)/shard_map/sums/pallas_call | solution.py:221
  3.4 0.1 collective-permute-start
  3.5 1.6 %collective-permute-start.1 = (f32[232,128]{1,0:T(8,128)S(1)}, f32[232,128]{1,0:T(8,128)S(1)}, u32[]{:S(2)}, u32[]{:S(2)}) collective-permute-start(f32[232,128]{1,0:T(8,128)S(1)} %get-tuple-element.30), channel_id=1, source_target_pairs={{0,2},{2,4},{4,6},{6,8},{8,10},{10,12},{12,14},{14,0},{1,3},{3,5},... | collective-permute-start | bytes 356360 | tf_op jit(solution)/shard_map/ppermute | solution.py:220
  5.1 0.5 %collective-permute-start.2 = (f32[232,128]{1,0:T(8,128)S(1)}, f32[232,128]{1,0:T(8,128)S(1)}, u32[]{:S(2)}, u32[]{:S(2)}) collective-permute-start(f32[232,128]{1,0:T(8,128)S(1)} %get-tuple-element.31), channel_id=1, source_target_pairs={{0,14},{2,0},{4,2},{6,4},{8,6},{10,8},{12,10},{14,12},{1,15},{3,1}... | collective-permute-start | bytes 356360 | tf_op jit(solution)/shard_map/ppermute | solution.py:219
  5.5 6.4 %collective-permute-start.3 = (f32[8,128]{1,0:T(8,128)S(1)}, f32[8,128]{1,0:T(8,128)S(1)}, u32[]{:S(2)}, u32[]{:S(2)}) collective-permute-start(f32[8,128]{1,0:T(8,128)S(1)} %get-tuple-element.32), channel_id=1, source_target_pairs={{2,12},{4,10},{10,4},{12,2},{3,13},{5,11},{11,5},{13,3},{18,28},{2... | collective-permute-start | bytes 12296 | tf_op jit(solution)/shard_map/ppermute | solution.py:218
  11.9 1.5 %inner.1 = f32[12,4,8,512]{3,2,1,0:T(8,128)S(1)} custom-call(f32[12]{0:T(128)S(1)} %get-tuple-element.29.decay, f32[12,4,8,512]{3,2,1,0:T(8,128)S(1)} %get-tuple-element.20.lam, f32[4,8,512]{2,1,0:T(8,128)S(1)} %get-tuple-element.21.vel_u, f32[4,8,512]{2,1,0:T(8,128)S(1)} %get-tuple-element.22.vel_v, f32[4,8,512]{2,1,0:T(8,128)S(1)} %get-tuple-element.23.kappa, ...), custom_call_target="tpu_custom_call" | custom-call | tf_op jit(solution)/shard_map/inner/pallas_call | solution.py:231
  13.4 0.0 collective-permute-done.sums_other
  13.4 1.3 %react.1.inner = f32[12,4,8,512]{3,2,1,0:T(8,128)S(1)} custom-call(f32[8,24]{1,0:T(8,128)S(1)} %get-tuple-element.25.w_in, f32[4,8,512]{2,1,0:T(8,128)S(1)} %get-tuple-element.26.light, s32[4,8,512]{2,1,0:T(8,128)S(1)} %get-tuple-element.24.sea_int.sea, f32[16,4,8,512]{3,2,1,0:T(8,128)S(1)} %sums.1, f32[16,4,8,512]{3,2,1,0:T(8,128)S(1)} %collective-permute-done.sums_other, ...), custom_call_target="tpu_custom_call" | custom-call | tf_op jit(solution)/shard_map/react/pallas_call | solution.py:240
  14.7 0.0 collective-permute-done.3.from_fold
  14.7 0.0 collective-permute-done.1.from_west
  14.7 0.0 collective-permute-done.2.from_east
  14.7 1.6 %edges.1 = f32[12,4,8,512]{3,2,1,0:T(8,128)} custom-call(s32[8]{0:T(128)S(1)} %get-tuple-element.19.partner, f32[12,4,8,512]{3,2,1,0:T(8,128)S(1)} %get-tuple-element.20.lam, f32[4,8,512]{2,1,0:T(8,128)S(1)} %get-tuple-element.21.vel_u, f32[4,8,512]{2,1,0:T(8,128)S(1)} %get-tuple-element.22.vel_v, f32[4,8,512]{2,1,0:T(8,128)S(1)} %get-tuple-element.23.kappa, ...), custom_call_target="tpu_custom_call" | custom-call | tf_op jit(solution)/shard_map/edges/pallas_call | solution.py:249
Async XLA Ops:
  3.4 10.0 %collective-permute-start = (f32[16,4,8,512]{3,2,1,0:T(8,128)S(1)}, f32[16,4,8,512]{3,2,1,0:T(8,128)S(1)}, u32[]{:S(2)}, u32[]{:S(2)}) collective-permute-start(f32[16,4,8,512]{3,2,1,0:T(8,128)S(1)} %sums.1), channel_id=1, source_target_pairs={{0,1},{1,0},{2,3},{3,2},{4,5},{5,4},{6,7},{7,6},{8,9},{9,8},{10,11... | collective-permute-start | bytes 3145736 | tf_op jit(solution)/shard_map/ppermute | solution.py:230
  3.5 11.2 %collective-permute-start.1 = (f32[232,128]{1,0:T(8,128)S(1)}, f32[232,128]{1,0:T(8,128)S(1)}, u32[]{:S(2)}, u32[]{:S(2)}) collective-permute-start(f32[232,128]{1,0:T(8,128)S(1)} %get-tuple-element.30), channel_id=1, source_target_pairs={{0,2},{2,4},{4,6},{6,8},{8,10},{10,12},{12,14},{14,0},{1,3},{3,5},... | collective-permute-start | bytes 356360 | tf_op jit(solution)/shard_map/ppermute | solution.py:220
  5.1 9.7 %collective-permute-start.2 = (f32[232,128]{1,0:T(8,128)S(1)}, f32[232,128]{1,0:T(8,128)S(1)}, u32[]{:S(2)}, u32[]{:S(2)}) collective-permute-start(f32[232,128]{1,0:T(8,128)S(1)} %get-tuple-element.31), channel_id=1, source_target_pairs={{0,14},{2,0},{4,2},{6,4},{8,6},{10,8},{12,10},{14,12},{1,15},{3,1}... | collective-permute-start | bytes 356360 | tf_op jit(solution)/shard_map/ppermute | solution.py:219
  5.5 9.2 %collective-permute-start.3 = (f32[8,128]{1,0:T(8,128)S(1)}, f32[8,128]{1,0:T(8,128)S(1)}, u32[]{:S(2)}, u32[]{:S(2)}) collective-permute-start(f32[8,128]{1,0:T(8,128)S(1)} %get-tuple-element.32), channel_id=1, source_target_pairs={{2,12},{4,10},{10,4},{12,2},{3,13},{5,11},{11,5},{13,3},{18,28},{2... | collective-permute-start | bytes 12296 | tf_op jit(solution)/shard_map/ppermute | solution.py:218

commit v2 on v1

v2 whole, which is shorter than its diff:
```python
import jax
import jax.numpy as jnp
from jax import lax
from jax.experimental import pallas as pl
from jax.experimental.pallas import tpu as pltpu
from jax.sharding import PartitionSpec as P

F32, BF16 = jnp.float32, jnp.bfloat16
VMEM = pl.BlockSpec(memory_space=pltpu.VMEM)
SMEM = pl.BlockSpec(memory_space=pltpu.SMEM)
HBM = pl.BlockSpec(memory_space=pltpu.HBM)
LANES = 128


def halves(x):
    high = x.astype(BF16)
    return high, (x - high.astype(F32)).astype(BF16)


def spread(target, weight, blocks, width, cols):
    lane = lax.broadcasted_iota(jnp.int32, (cols, width * cols), 1)
    sub = lax.broadcasted_iota(jnp.int32, (cols, width * cols), 0)
    square, diagonal = lane // cols, lane % cols == sub
    chosen = [square == other for other in range(width)]
    high, low = [], []
    for block in range(blocks):
        row = jnp.zeros((cols, width * cols), F32)
        for other in range(width):
            row = jnp.where(chosen[other], weight(block, other), row)
        row = jnp.where(diagonal, row, 0.0)
        top = row.astype(BF16).astype(F32)
        high.append(top)
        low.append(row - top)
    target[...] = jnp.concatenate(high + low, axis=0).astype(BF16)


def product(matrix, x):
    half = matrix.shape[0] // 2
    high, low = halves(x)
    first = jnp.dot(matrix[...], high, preferred_element_type=F32)
    return first[:half] + first[half:] + jnp.dot(matrix[:half], low, preferred_element_type=F32)


def pack_kernel(
    w_in_hbm, w_out_hbm, decay_hbm, partner_hbm, vel_u_hbm, vel_v_hbm, kappa_hbm, sea_hbm, lam_hbm, tracers_hbm, light_hbm,
    vel_u, vel_v, kappa, sea, lam, tracers, light, pack_east, pack_west, top_out, to_uptake, to_weighted, to_tracers, fade, order,
    w_in, w_out, decay, partner, sems,
):
    count, levels, cols, rows = lam.shape
    edge = count * levels
    tall = edge + 2 * levels
    reactions = w_in.shape[0]
    sources = (w_in_hbm, w_out_hbm, decay_hbm, partner_hbm, vel_u_hbm, vel_v_hbm, kappa_hbm, sea_hbm, lam_hbm, tracers_hbm, light_hbm)
    targets = (w_in, w_out, decay, partner, vel_u, vel_v, kappa, sea, lam, tracers, light)
    copies = [pltpu.make_async_copy(s, t, sems.at[i]) for i, (s, t) in enumerate(zip(sources, targets))]
    for copy in copies:
        copy.start()
    first = lax.axis_index("tracer") * count
    for copy in copies[:4]:
        copy.wait()
    for a in range(count):
        fade[pl.ds(a, 1), :] = jnp.full((1, rows), decay[a], F32)
    sub = lax.broadcasted_iota(jnp.int32, (cols, LANES), 0)
    picks = jnp.zeros((cols, LANES), jnp.int32)
    for i in range(cols):
        picks = jnp.where(sub == i, lax.rem(partner[i], cols), picks)
    order[...] = picks
    spread(to_uptake, lambda h, a: w_in[h, first + a], reactions, count, cols)
    spread(to_weighted, lambda h, a: w_out[h, first + a], reactions, count, cols)
    spread(to_tracers, lambda a, h: w_in[h, first + a], count, reactions, cols)
    for copy in copies[4:9]:
        copy.wait()

    for target, line, sign in ((pack_east, slice(cols - 1, cols), -0.5), (pack_west, slice(0, 1), 0.5)):

        def put(index, value):
            for c in range(rows // LANES):
                target[pl.ds(c * tall + index, 1), :] = value[:, c * LANES : (c + 1) * LANES]

        for a in range(count):
            for k in range(levels):
                put(a * levels + k, lam[a, k, line, :])
        for k in range(levels):
            put(edge + k, 0.25 * vel_u[k, line, :] + sign * kappa[k, line, :])
            put(edge + levels + k, sea[k, line, :].astype(F32))

    lane = lax.broadcasted_iota(jnp.int32, (cols, LANES), 1)
    top = jnp.zeros((cols, LANES), F32)
    last = rows - LANES

    def placed(top, index, value):
        return jnp.where(lane == index, pltpu.roll(value, index + 1, 1), top)

    for a in range(count):
        for k in range(levels):
            top = placed(top, a * levels + k, lam[a, k, :, last:])
    for k in range(levels):
        top = placed(top, edge + k, 0.5 * kappa[k, :, last:] - 0.25 * vel_v[k, :, last:])
        top = placed(top, edge + levels + k, sea[k, :, last:].astype(F32))
    for target in (pack_east, pack_west):
        target[pl.ds(rows // LANES * tall, cols), :] = top
    top_out[...] = top
    for copy in copies[9:]:
        copy.wait()


def sums_kernel(to_uptake, to_weighted, lam, tracers, sums):
    count, levels, cols, rows = lam.shape
    reactions = sums.shape[0] // 2
    for k in range(levels):
        for field, matrix, base in ((tracers, to_uptake, 0), (lam, to_weighted, reactions)):
            total = product(matrix, field[:, k].reshape(count * cols, rows))
            sums[pl.ds(base, reactions), k] = total.reshape(reactions, cols, rows)


def inner_kernel(fade, lam, vel_u, vel_v, kappa, sea_int, top, out, top_out):
    count, levels, cols, rows = lam.shape
    col = lax.broadcasted_iota(jnp.int32, (cols, rows), 0)
    row = lax.broadcasted_iota(jnp.int32, (cols, rows), 1)

    def level(k, carry):
        sea = sea_int[k].astype(F32)
        u, v, kap = 0.25 * vel_u[k], 0.25 * vel_v[k], 0.5 * kappa[k]
        east = jnp.where(col == cols - 1, 0.0, sea * pltpu.roll(sea, cols - 1, 0))
        north = jnp.where(row == rows - 1, 0.0, sea * pltpu.roll(sea, rows - 1, 1))
        p, q = u + kap, u - kap
        pn, qn = v + kap, v - kap
        c_e = east * (p + pltpu.roll(p, cols - 1, 0))
        c_w = pltpu.roll(east * (q + pltpu.roll(q, cols - 1, 0)), 1, 0)
        c_n = north * (pn + pltpu.roll(pn, rows - 1, 1))
        c_s = pltpu.roll(north * (qn + pltpu.roll(qn, rows - 1, 1)), 1, 1)
        own = sea + (c_w + c_s - c_e - c_n)
        for a in range(count):
            x = lam[a, k]
            y = (own - fade[pl.ds(a, 1), :] * sea) * x
            y += c_e * pltpu.roll(x, cols - 1, 0)
            y -= c_w * pltpu.roll(x, 1, 0)
            y += c_n * pltpu.roll(x, rows - 1, 1)
            y -= c_s * pltpu.roll(x, 1, 1)
            out[a, k] = y
        return carry

    top_out[...] = top[...]
    lax.fori_loop(0, levels, level, 0)


def react_kernel(to_tracers, light, sea, sums, sums_other, inner, out):
    count, levels, cols, rows = inner.shape
    reactions = sums.shape[0] // 2
    for k in range(levels):
        lit = light[k] * sea[k].astype(F32)
        gain = []
        for h in range(reactions):
            t = jnp.tanh(sums[h, k] + sums_other[h, k])
            gain.append(lit * (1.0 - t * t) * (sums[reactions + h, k] + sums_other[reactions + h, k]))
        coupled = product(to_tracers, jnp.concatenate(gain, axis=0))
        out[:, k] = inner[:, k] + coupled.reshape(count, cols, rows)


def edges_kernel(
    order, lam, vel_u, vel_v, kappa, sea_int, inner, from_west, from_east, from_fold, out_hbm,
    out, sems,
):
    count, levels, cols, rows = lam.shape
    edge = count * levels
    tall = edge + 2 * levels
    chunks = rows // LANES
    place, strips = lax.axis_index("space"), lax.axis_size("space")
    to_east, to_west = lax.rem(place + 1, strips), lax.rem(place + strips - 1, strips)
    mirror = strips - 1 - place
    at_fold = pl.ds(chunks * tall, cols)
    fold_rows = jnp.where(mirror == to_east, from_east[at_fold, :], from_fold[...])
    fold_rows = jnp.where(mirror == to_west, from_west[at_fold, :], fold_rows)
    across = jnp.zeros((cols, LANES), F32)
    for p in range(cols):
        across = jnp.where(order[...] == p, fold_rows[p : p + 1, :], across)
    sub = lax.broadcasted_iota(jnp.int32, (cols, LANES), 0)
    lane = lax.broadcasted_iota(jnp.int32, (cols, LANES), 1)
    side = jnp.where(sub == 0, -1.0, jnp.where(sub == cols - 1, 1.0, 0.0))

    def beyond(c, index):
        at = pl.ds(c * tall + index, 1)
        return jnp.where(sub == 0, from_west[at, :], from_east[at, :])

    def folded_at(index):
        return pltpu.roll(across, LANES - 1 - index, 1)

    def copy(k):
        return pltpu.make_async_copy(out.at[:, k], out_hbm.at[:, k], sems.at[k])

    def level(k, carry):
        for c in range(chunks):
            part = slice(c * LANES, (c + 1) * LANES)
            sea, u, kap = sea_int[k, :, part].astype(F32), 0.25 * vel_u[k, :, part], 0.5 * kappa[k, :, part]
            mine = jnp.where(sub == 0, u - kap, u + kap)
            coef = side * sea * beyond(c, edge + levels + k) * (mine + beyond(c, edge + k))
            if c == chunks - 1:
                up = 0.25 * vel_v[k, :, part] + kap + folded_at(edge + k)
                fold = jnp.where(lane == LANES - 1, sea * folded_at(edge + levels + k) * up, 0.0)
            for a in range(count):
                x = lam[a, k, :, part]
                y = inner[a, k, :, part] + coef * (beyond(c, a * levels + k) - x)
                if c == chunks - 1:
                    y += fold * (folded_at(a * levels + k) - x)
                out[a, k, :, part] = y
        copy(k).start()
        return carry

    lax.fori_loop(0, levels, level, 0)
    for k in range(levels):
        copy(k).wait()


def cost(flops, count):
    return pl.CostEstimate(flops=0, bytes_accessed=0, transcendentals=0)


def body(lam, tracers, vel_u, vel_v, kappa, light, sea_int, partner, decay, w_in, w_out):
    count, levels, cols, rows = lam.shape
    reactions = w_in.shape[0]
    tall = (count + 2) * levels * (rows // LANES)
    n = lax.axis_size("space")
    params = pltpu.CompilerParams(vmem_limit_bytes=32 << 20)
    whole = jax.ShapeDtypeStruct(lam.shape, F32)
    shares = jax.ShapeDtypeStruct((2 * reactions, levels, cols, rows), F32)
    tile = jax.ShapeDtypeStruct((cols, LANES), F32)
    scalars = (w_in, w_out.T, decay, partner)
    arguments = (vel_u, vel_v, kappa, sea_int, lam, tracers, light)
    vel_u, vel_v, kappa, sea_int, lam, tracers, light, pack_east, pack_west, top, to_uptake, to_weighted, to_tracers, fade, order = pl.pallas_call(
        pack_kernel,
        name="pack",
        out_shape=(
            *(jax.ShapeDtypeStruct(x.shape, x.dtype) for x in arguments),
            jax.ShapeDtypeStruct((tall + cols, LANES), F32),
            jax.ShapeDtypeStruct((tall + cols, LANES), F32),
            tile,
            *[jax.ShapeDtypeStruct((2 * reactions * cols, count * cols), BF16)] * 2,
            jax.ShapeDtypeStruct((2 * count * cols, reactions * cols), BF16),
            jax.ShapeDtypeStruct((count, rows), F32),
            jax.ShapeDtypeStruct((cols, LANES), jnp.int32),
        ),
        in_specs=[HBM] * 11,
        out_specs=(VMEM,) * 15,
        scratch_shapes=[*(pltpu.SMEM(x.shape, x.dtype) for x in scalars), pltpu.SemaphoreType.DMA((11,))],
        compiler_params=params,
        cost_estimate=cost(0, 4 * lam.size),
    )(*(pltpu.with_memory_space_constraint(x, pltpu.HBM) for x in scalars + arguments))
    eastward = [(s, (s + 1) % n) for s in range(n)]
    westward = [(s, (s - 1) % n) for s in range(n)]
    mirrored = [(s, n - 1 - s) for s in range(n)]
    from_east = lax.ppermute(pack_west, "space", westward)
    from_west = lax.ppermute(pack_east, "space", eastward)
    sums = pl.pallas_call(
        sums_kernel,
        name="sums",
        out_shape=shares,
        in_specs=[VMEM] * 4,
        out_specs=VMEM,
        compiler_params=params,
        cost_estimate=cost(32 * lam.size, 4 * lam.size),
    )(to_uptake, to_weighted, lam, tracers)
    sums_other = lax.ppermute(sums, "tracer", [(0, 1), (1, 0)])
    inner, top = pl.pallas_call(
        inner_kernel,
        name="inner",
        out_shape=(whole, tile),
        in_specs=[VMEM] * 7,
        out_specs=(VMEM, VMEM),
        compiler_params=params,
        cost_estimate=cost(10 * lam.size, 4 * lam.size),
    )(fade, lam, vel_u, vel_v, kappa, sea_int, top)
    from_fold = lax.ppermute(top, "space", [p for p in mirrored if p not in eastward + westward])
    inner = pl.pallas_call(
        react_kernel,
        name="react",
        out_shape=whole,
        in_specs=[VMEM] * 6,
        out_specs=VMEM,
        compiler_params=params,
        cost_estimate=cost(16 * lam.size, 4 * lam.size),
    )(to_tracers, light, sea_int, sums, sums_other, inner)
    return pl.pallas_call(
        edges_kernel,
        name="edges",
        out_shape=whole,
        in_specs=[VMEM] * 10,
        out_specs=HBM,
        scratch_shapes=[
            pltpu.VMEM(lam.shape, F32),
            pltpu.SemaphoreType.DMA((levels,)),
        ],
        compiler_params=params,
        cost_estimate=cost(10 * lam.size, 4 * lam.size),
    )(order, lam, vel_u, vel_v, kappa, sea_int, inner, from_west, from_east, from_fold)


def solution(mesh):
    placed = (
        P(("member", "tracer"), None, "space", None),
        P(("member", "tracer"), None, "space", None),
        P("member", "space", None),
        P("member", "space", None),
        P("member", "space", None),
        P("member", "space", None),
        P(None, "space", None),
        P("space"),
        P("tracer"),
        P(),
        P(),
    )
    return jax.shard_map(
        body,
        mesh=mesh,
        in_specs=placed,
        out_specs=P(("member", "tracer"), None, "space", None),
        check_vma=False,
    )
```

time: 16.5 us -> 15.6 us (0.945)
  the two profiles are of different devices: /device:TPU:2 before, /device:TPU:24 now
where the time goes in v2:
time: 15.6 us; the launch traced here: 15.5 us
  waiting for transfers between devices  5.52 us (35%)
  starting transfers between devices  5.21 us (33%)
  Pallas kernels  4.69 us (30%)
    ppermute x1, waiting for transfers between devices, body(): lax.ppermute(top, 'space', [p for p in mirrored if p not in eastward + we...  5.51 us
    ppermute x1, starting transfers between devices, body(): lax.ppermute(top, 'space', [p for p in mirrored if p not in eastward + we...  2.16 us
    pallas_call x1, Pallas kernels, body(): pl.pallas_call(pack_kernel, name='pack', out_shape=(*(jax.ShapeDtypeStruc...  1.65 us
    ppermute x1, starting transfers between devices, body(): from_west = lax.ppermute(pack_east, 'space', eastward)  1.54 us
    ppermute x1, starting transfers between devices, body(): from_east = lax.ppermute(pack_west, 'space', westward)  1.43 us
    pallas_call x1, Pallas kernels, body(): pl.pallas_call(edges_kernel, name='edges', out_shape=whole, in_specs=[VME...  1.07 us
    pallas_call x1, Pallas kernels, body(): pl.pallas_call(inner_kernel, name='inner', out_shape=(whole, tile), in_sp...  0.9 us
    pallas_call x1, Pallas kernels, body(): pl.pallas_call(sums_kernel, name='sums', out_shape=shares, in_specs=[VMEM...  0.57 us
  transfers between devices with their start and end apart: 4, of which 1 were waited for; matrix products, arithmetic and copies ran while one was open for 0% of the time, Pallas kernels for 9%

profile of v2, /device:TPU:24, one launch (start us, length us, event | category | flops | bytes accessed | tf_op | source)
XLA Modules:
  0.0 15.5 jit_solution(16307190186570975737)
XLA Ops:
  0.0 1.6 %pack.1 = (f32[4,8,512]{2,1,0:T(8,128)S(1)}, f32[4,8,512]{2,1,0:T(8,128)S(1)}, f32[4,8,512]{2,1,0:T(8,128)S(1)}, s32[4,8,512]{2,1,0:T(8,128)S(1)}, f32[12,4,8,51...) custom-call(f32[8,24]{1,0:T(8,128)} %w_in_hbm.1, ...), custom_call_target="tpu_custom_call" | custom-call | tf_op jit(solution)/shard_map/pack/pallas_call | solution.py:229
  1.7 0.6 %sums.1 = f32[16,4,8,512]{3,2,1,0:T(8,128)S(1)} custom-call(bf16[128,96]{1,0:T(8,128)(2,1)S(1)} %get-tuple-element.30.to_uptake, bf16[128,96]{1,0:T(8,128)(2,1)S(1)} %get-tuple-element.31.to_weighted, f32[12,4,8,512]{3,2,1,0:T(8,128)S(1)} %get-tuple-element.23.lam, f32[12,4,8,512]{3,2,1,0:T(8,128)S(1)} %get-tuple-element.32.tracers), custom_call_target="tpu_custom_call" | custom-call | tf_op jit(solution)/shard_map/sums/pallas_call | solution.py:253
  2.2 0.1 collective-permute-start
  2.3 1.5 %collective-permute-start.1 = (f32[232,128]{1,0:T(8,128)S(1)}, f32[232,128]{1,0:T(8,128)S(1)}, u32[]{:S(2)}, u32[]{:S(2)}) collective-permute-start(f32[232,128]{1,0:T(8,128)S(1)} %get-tuple-element.36), channel_id=1, source_target_pairs={{0,2},{2,4},{4,6},{6,8},{8,10},{10,12},{12,14},{14,0},{1,3},{3,5},... | collective-permute-start | bytes 356360 | tf_op jit(solution)/shard_map/ppermute | solution.py:252
  3.8 1.4 %collective-permute-start.2 = (f32[232,128]{1,0:T(8,128)S(1)}, f32[232,128]{1,0:T(8,128)S(1)}, u32[]{:S(2)}, u32[]{:S(2)}) collective-permute-start(f32[232,128]{1,0:T(8,128)S(1)} %get-tuple-element.37), channel_id=1, source_target_pairs={{0,14},{2,0},{4,2},{6,4},{8,6},{10,8},{12,10},{14,12},{1,15},{3,1}... | collective-permute-start | bytes 356360 | tf_op jit(solution)/shard_map/ppermute | solution.py:251
  5.3 0.9 %inner.1 = (f32[12,4,8,512]{3,2,1,0:T(8,128)S(1)}, f32[8,128]{1,0:T(8,128)S(1)}) custom-call(f32[12,512]{1,0:T(8,128)S(1)} %get-tuple-element.33.fade, f32[12,4,8,512]{3,2,1,0:T(8,128)S(1)} %get-tuple-element.23.lam, f32[4,8,512]{2,1,0:T(8,128)S(1)} %get-tuple-element.24.vel_u, f32[4,8,512]{2,1,0:T(8,128)S(1)} %get-tuple-element.25.vel_v, ...), custom_call_target="tpu_custom_call" | custom-call | tf_op jit(solution)/shard_map/inner/pallas_call | solution.py:263
  6.2 2.2 %collective-permute-start.3 = (f32[8,128]{1,0:T(8,128)S(1)}, f32[8,128]{1,0:T(8,128)S(1)}, u32[]{:S(2)}, u32[]{:S(2)}) collective-permute-start(f32[8,128]{1,0:T(8,128)S(1)} %get-tuple-element.38), channel_id=1, source_target_pairs={{2,12},{4,10},{10,4},{12,2},{3,13},{5,11},{11,5},{13,3},{18,28},{2... | collective-permute-start | bytes 12296 | tf_op jit(solution)/shard_map/ppermute | solution.py:272
  8.4 0.0 collective-permute-done.sums_other
  8.4 0.5 %react.1.inner = f32[12,4,8,512]{3,2,1,0:T(8,128)S(1)} custom-call(bf16[192,64]{1,0:T(8,128)(2,1)S(1)} %get-tuple-element.28.to_tracers, f32[4,8,512]{2,1,0:T(8,128)S(1)} %get-tuple-element.29.light, s32[4,8,512]{2,1,0:T(8,128)S(1)} %get-tuple-element.27.sea_int.sea, f32[16,4,8,512]{3,2,1,0:T(8,128)S(1)} %sums.1, ...), custom_call_target="tpu_custom_call" | custom-call | tf_op jit(solution)/shard_map/react/pallas_call | solution.py:273
  8.9 5.5 %collective-permute-done.3.from_fold = f32[8,128]{1,0:T(8,128)S(1)} collective-permute-done((f32[8,128]{1,0:T(8,128)S(1)}, f32[8,128]{1,0:T(8,128)S(1)}, u32[]{:S(2)}, u32[]{:S(2)}) %collective-permute-start.3) | collective-permute-done | bytes 4128 | tf_op jit(solution)/shard_map/ppermute | solution.py:272
  14.4 0.0 collective-permute-done.1.from_west
  14.4 0.0 collective-permute-done.2.from_east
  14.4 1.1 %edges.1 = f32[12,4,8,512]{3,2,1,0:T(8,128)} custom-call(s32[8,128]{1,0:T(8,128)S(1)} %get-tuple-element.22.order, f32[12,4,8,512]{3,2,1,0:T(8,128)S(1)} %get-tuple-element.23.lam, f32[4,8,512]{2,1,0:T(8,128)S(1)} %get-tuple-element.24.vel_u, f32[4,8,512]{2,1,0:T(8,128)S(1)} %get-tuple-element.25.vel_v, f32[4,8,512]{2,1,0:T(8,128)S(1)} %get-tuple-element.26.kappa, ...), custom_call_target="tpu_custom_call" | custom-call | tf_op jit(solution)/shard_map/edges/pallas_call | solution.py:282
Async XLA Ops:
  2.2 6.1 %collective-permute-start = (f32[16,4,8,512]{3,2,1,0:T(8,128)S(1)}, f32[16,4,8,512]{3,2,1,0:T(8,128)S(1)}, u32[]{:S(2)}, u32[]{:S(2)}) collective-permute-start(f32[16,4,8,512]{3,2,1,0:T(8,128)S(1)} %sums.1), channel_id=1, source_target_pairs={{0,1},{1,0},{2,3},{3,2},{4,5},{5,4},{6,7},{7,6},{8,9},{9,8},{10,11... | collective-permute-start | bytes 3145736 | tf_op jit(solution)/shard_map/ppermute | solution.py:262
  2.3 12.1 %collective-permute-start.1 = (f32[232,128]{1,0:T(8,128)S(1)}, f32[232,128]{1,0:T(8,128)S(1)}, u32[]{:S(2)}, u32[]{:S(2)}) collective-permute-start(f32[232,128]{1,0:T(8,128)S(1)} %get-tuple-element.36), channel_id=1, source_target_pairs={{0,2},{2,4},{4,6},{6,8},{8,10},{10,12},{12,14},{14,0},{1,3},{3,5},... | collective-permute-start | bytes 356360 | tf_op jit(solution)/shard_map/ppermute | solution.py:252
  3.8 10.6 %collective-permute-start.2 = (f32[232,128]{1,0:T(8,128)S(1)}, f32[232,128]{1,0:T(8,128)S(1)}, u32[]{:S(2)}, u32[]{:S(2)}) collective-permute-start(f32[232,128]{1,0:T(8,128)S(1)} %get-tuple-element.37), channel_id=1, source_target_pairs={{0,14},{2,0},{4,2},{6,4},{8,6},{10,8},{12,10},{14,12},{1,15},{3,1}... | collective-permute-start | bytes 356360 | tf_op jit(solution)/shard_map/ppermute | solution.py:251
  6.2 8.2 %collective-permute-start.3 = (f32[8,128]{1,0:T(8,128)S(1)}, f32[8,128]{1,0:T(8,128)S(1)}, u32[]{:S(2)}, u32[]{:S(2)}) collective-permute-start(f32[8,128]{1,0:T(8,128)S(1)} %get-tuple-element.38), channel_id=1, source_target_pairs={{2,12},{4,10},{10,4},{12,2},{3,13},{5,11},{11,5},{13,3},{18,28},{2... | collective-permute-start | bytes 12296 | tf_op jit(solution)/shard_map/ppermute | solution.py:272

commit v3 on v2

--- a/solution.py
+++ b/solution.py
@@ -43,9 +43,10 @@
 
 def pack_kernel(
     w_in_hbm, w_out_hbm, decay_hbm, partner_hbm, vel_u_hbm, vel_v_hbm, kappa_hbm, sea_hbm, lam_hbm, tracers_hbm, light_hbm,
-    vel_u, vel_v, kappa, sea, lam, tracers, light, pack_east, pack_west, top_out, to_uptake, to_weighted, to_tracers, fade, order,
+    vel_u, vel_v, kappa, sea, light, both, pack_east, pack_west, top_out, to_uptake, to_weighted, to_uptake_other, to_weighted_other, to_tracers, fade, order,
     w_in, w_out, decay, partner, sems,
 ):
+    lam, tracers = both.at[0], both.at[1]
     count, levels, cols, rows = lam.shape
     edge = count * levels
     tall = edge + 2 * levels
@@ -67,6 +68,9 @@
     order[...] = picks
     spread(to_uptake, lambda h, a: w_in[h, first + a], reactions, count, cols)
     spread(to_weighted, lambda h, a: w_out[h, first + a], reactions, count, cols)
+    second = count - first
+    spread(to_uptake_other, lambda h, a: w_in[h, second + a], reactions, count, cols)
+    spread(to_weighted_other, lambda h, a: w_out[h, second + a], reactions, count, cols)
     spread(to_tracers, lambda a, h: w_in[h, first + a], count, reactions, cols)
     for copy in copies[4:9]:
         copy.wait()
@@ -104,16 +108,17 @@
         copy.wait()
 
 
-def sums_kernel(to_uptake, to_weighted, lam, tracers, sums):
-    count, levels, cols, rows = lam.shape
+def sums_kernel(to_uptake, to_weighted, both, sums):
+    _, count, levels, cols, rows = both.shape
     reactions = sums.shape[0] // 2
     for k in range(levels):
-        for field, matrix, base in ((tracers, to_uptake, 0), (lam, to_weighted, reactions)):
-            total = product(matrix, field[:, k].reshape(count * cols, rows))
+        for field, matrix, base in ((1, to_uptake, 0), (0, to_weighted, reactions)):
+            total = product(matrix, both[field, :, k].reshape(count * cols, rows))
             sums[pl.ds(base, reactions), k] = total.reshape(reactions, cols, rows)
 
 
-def inner_kernel(fade, lam, vel_u, vel_v, kappa, sea_int, top, out, top_out):
+def inner_kernel(fade, both, vel_u, vel_v, kappa, sea_int, out):
+    lam = both.at[0]
     count, levels, cols, rows = lam.shape
     col = lax.broadcasted_iota(jnp.int32, (cols, rows), 0)
     row = lax.broadcasted_iota(jnp.int32, (cols, rows), 1)
@@ -140,27 +145,30 @@
             out[a, k] = y
         return carry
 
-    top_out[...] = top[...]
     lax.fori_loop(0, levels, level, 0)
 
 
-def react_kernel(to_tracers, light, sea, sums, sums_other, inner, out):
+def react_kernel(to_uptake, to_weighted, to_tracers, light, sea, sums, both, inner, out):
     count, levels, cols, rows = inner.shape
     reactions = sums.shape[0] // 2
     for k in range(levels):
         lit = light[k] * sea[k].astype(F32)
+        uptake = product(to_uptake, both[1, :, k].reshape(count * cols, rows))
+        weighted = product(to_weighted, both[0, :, k].reshape(count * cols, rows))
         gain = []
         for h in range(reactions):
-            t = jnp.tanh(sums[h, k] + sums_other[h, k])
-            gain.append(lit * (1.0 - t * t) * (sums[reactions + h, k] + sums_other[reactions + h, k]))
+            part = slice(h * cols, (h + 1) * cols)
+            t = jnp.tanh(sums[h, k] + uptake[part])
+            gain.append(lit * (1.0 - t * t) * (sums[reactions + h, k] + weighted[part]))
         coupled = product(to_tracers, jnp.concatenate(gain, axis=0))
         out[:, k] = inner[:, k] + coupled.reshape(count, cols, rows)
 
 
 def edges_kernel(
-    order, lam, vel_u, vel_v, kappa, sea_int, inner, from_west, from_east, from_fold, out_hbm,
+    order, both, vel_u, vel_v, kappa, sea_int, inner, from_west, from_east, from_fold, out_hbm,
     out, sems,
 ):
+    lam = both.at[0]
     count, levels, cols, rows = lam.shape
     edge = count * levels
     tall = edge + 2 * levels
@@ -226,21 +234,23 @@
     tile = jax.ShapeDtypeStruct((cols, LANES), F32)
     scalars = (w_in, w_out.T, decay, partner)
     arguments = (vel_u, vel_v, kappa, sea_int, lam, tracers, light)
-    vel_u, vel_v, kappa, sea_int, lam, tracers, light, pack_east, pack_west, top, to_uptake, to_weighted, to_tracers, fade, order = pl.pallas_call(
+    whole = jax.ShapeDtypeStruct(lam.shape, F32)
+    vel_u, vel_v, kappa, sea_int, light, both, pack_east, pack_west, top, *spreads, to_tracers, fade, order = pl.pallas_call(
         pack_kernel,
         name="pack",
         out_shape=(
-            *(jax.ShapeDtypeStruct(x.shape, x.dtype) for x in arguments),
+            *(jax.ShapeDtypeStruct(x.shape, x.dtype) for x in (vel_u, vel_v, kappa, sea_int, light)),
+            jax.ShapeDtypeStruct((2, *lam.shape), F32),
             jax.ShapeDtypeStruct((tall + cols, LANES), F32),
             jax.ShapeDtypeStruct((tall + cols, LANES), F32),
             tile,
-            *[jax.ShapeDtypeStruct((2 * reactions * cols, count * cols), BF16)] * 2,
+            *[jax.ShapeDtypeStruct((2 * reactions * cols, count * cols), BF16)] * 4,
             jax.ShapeDtypeStruct((2 * count * cols, reactions * cols), BF16),
             jax.ShapeDtypeStruct((count, rows), F32),
             jax.ShapeDtypeStruct((cols, LANES), jnp.int32),
         ),
         in_specs=[HBM] * 11,
-        out_specs=(VMEM,) * 15,
+        out_specs=(VMEM,) * 16,
         scratch_shapes=[*(pltpu.SMEM(x.shape, x.dtype) for x in scalars), pltpu.SemaphoreType.DMA((11,))],
         compiler_params=params,
         cost_estimate=cost(0, 4 * lam.size),
@@ -248,37 +258,37 @@
     eastward = [(s, (s + 1) % n) for s in range(n)]
     westward = [(s, (s - 1) % n) for s in range(n)]
     mirrored = [(s, n - 1 - s) for s in range(n)]
+    from_fold = lax.ppermute(top, "space", [p for p in mirrored if p not in eastward + westward])
     from_east = lax.ppermute(pack_west, "space", westward)
     from_west = lax.ppermute(pack_east, "space", eastward)
     sums = pl.pallas_call(
         sums_kernel,
         name="sums",
         out_shape=shares,
-        in_specs=[VMEM] * 4,
+        in_specs=[VMEM] * 3,
         out_specs=VMEM,
         compiler_params=params,
         cost_estimate=cost(32 * lam.size, 4 * lam.size),
-    )(to_uptake, to_weighted, lam, tracers)
-    sums_other = lax.ppermute(sums, "tracer", [(0, 1), (1, 0)])
-    inner, top = pl.pallas_call(
+    )(*spreads[:2], both)
+    both_other = lax.ppermute(both, "tracer", [(0, 1), (1, 0)])
+    inner = pl.pallas_call(
         inner_kernel,
         name="inner",
-        out_shape=(whole, tile),
-        in_specs=[VMEM] * 7,
-        out_specs=(VMEM, VMEM),
+        out_shape=whole,
+        in_specs=[VMEM] * 6,
+        out_specs=VMEM,
         compiler_params=params,
         cost_estimate=cost(10 * lam.size, 4 * lam.size),
-    )(fade, lam, vel_u, vel_v, kappa, sea_int, top)
-    from_fold = lax.ppermute(top, "space", [p for p in mirrored if p not in eastward + westward])
+    )(fade, both, vel_u, vel_v, kappa, sea_int)
     inner = pl.pallas_call(
         react_kernel,
         name="react",
         out_shape=whole,
-        in_specs=[VMEM] * 6,
+        in_specs=[VMEM] * 8,
         out_specs=VMEM,
         compiler_params=params,
         cost_estimate=cost(16 * lam.size, 4 * lam.size),
-    )(to_tracers, light, sea_int, sums, sums_other, inner)
+    )(*spreads[2:], to_tracers, light, sea_int, sums, both_other, inner)
     return pl.pallas_call(
         edges_kernel,
         name="edges",
@@ -291,7 +301,7 @@
         ],
         compiler_params=params,
         cost_estimate=cost(10 * lam.size, 4 * lam.size),
-    )(order, lam, vel_u, vel_v, kappa, sea_int, inner, from_west, from_east, from_fold)
+    )(order, both, vel_u, vel_v, kappa, sea_int, inner, from_west, from_east, from_fold)
 
 
 def solution(mesh):

time: 15.6 us -> 14.4 us (0.923)
  the two profiles are of different devices: /device:TPU:24 before, /device:TPU:2 now
where the time goes in v3:
time: 14.4 us; the launch traced here: 14.2 us
  starting transfers between devices  8.52 us (59%)
  Pallas kernels  5.64 us (39%)
    ppermute x1, starting transfers between devices, body(): lax.ppermute(top, 'space', [p for p in mirrored if p not in eastward + we...  6.37 us
    pallas_call x1, Pallas kernels, body(): pl.pallas_call(pack_kernel, name='pack', out_shape=(*(jax.ShapeDtypeStruc...  1.69 us
    ppermute x1, starting transfers between devices, body(): from_west = lax.ppermute(pack_east, 'space', eastward)  1.6 us
    pallas_call x1, Pallas kernels, body(): pl.pallas_call(react_kernel, name='react', out_shape=whole, in_specs=[VME...  1.39 us
    pallas_call x1, Pallas kernels, body(): pl.pallas_call(edges_kernel, name='edges', out_shape=whole, in_specs=[VME...  1.09 us
    pallas_call x1, Pallas kernels, body(): pl.pallas_call(inner_kernel, name='inner', out_shape=whole, in_specs=[VME...  0.91 us
    pallas_call x1, Pallas kernels, body(): pl.pallas_call(sums_kernel, name='sums', out_shape=shares, in_specs=[VMEM...  0.56 us
    ppermute x1, starting transfers between devices, body(): from_east = lax.ppermute(pack_west, 'space', westward)  0.48 us
  transfers between devices with their start and end apart: 4, of which 0 were waited for; matrix products, arithmetic and copies ran while one was open for 0% of the time, Pallas kernels for 20%

profile of v3, /device:TPU:2, one launch (start us, length us, event | category | flops | bytes accessed | tf_op | source)
XLA Modules:
  0.0 14.2 jit_solution(13769502890834840220)
XLA Ops:
  0.0 1.7 %pack.1 = (f32[4,8,512]{2,1,0:T(8,128)S(1)}, f32[4,8,512]{2,1,0:T(8,128)S(1)}, f32[4,8,512]{2,1,0:T(8,128)S(1)}, s32[4,8,512]{2,1,0:T(8,128)S(1)}, f32[4,8,512]{...) custom-call(f32[8,24]{1,0:T(8,128)} %w_in_hbm.1, ...), custom_call_target="tpu_custom_call" | custom-call | tf_op jit(solution)/shard_map/pack/pallas_call | solution.py:238
  1.7 0.1 collective-permute-start
  1.8 1.6 %collective-permute-start.1 = (f32[232,128]{1,0:T(8,128)S(1)}, f32[232,128]{1,0:T(8,128)S(1)}, u32[]{:S(2)}, u32[]{:S(2)}) collective-permute-start(f32[232,128]{1,0:T(8,128)S(1)} %get-tuple-element.34), channel_id=1, source_target_pairs={{0,2},{2,4},{4,6},{6,8},{8,10},{10,12},{12,14},{14,0},{1,3},{3,5},... | collective-permute-start | bytes 356360 | tf_op jit(solution)/shard_map/ppermute | solution.py:263
  3.4 0.5 %collective-permute-start.2 = (f32[232,128]{1,0:T(8,128)S(1)}, f32[232,128]{1,0:T(8,128)S(1)}, u32[]{:S(2)}, u32[]{:S(2)}) collective-permute-start(f32[232,128]{1,0:T(8,128)S(1)} %get-tuple-element.35), channel_id=1, source_target_pairs={{0,14},{2,0},{4,2},{6,4},{8,6},{10,8},{12,10},{14,12},{1,15},{3,1}... | collective-permute-start | bytes 356360 | tf_op jit(solution)/shard_map/ppermute | solution.py:262
  3.9 6.4 %collective-permute-start.3 = (f32[8,128]{1,0:T(8,128)S(1)}, f32[8,128]{1,0:T(8,128)S(1)}, u32[]{:S(2)}, u32[]{:S(2)}) collective-permute-start(f32[8,128]{1,0:T(8,128)S(1)} %get-tuple-element.36), channel_id=1, source_target_pairs={{2,12},{4,10},{10,4},{12,2},{3,13},{5,11},{11,5},{13,3},{18,28},{2... | collective-permute-start | bytes 12296 | tf_op jit(solution)/shard_map/ppermute | solution.py:261
  10.2 0.6 %sums.1 = f32[16,4,8,512]{3,2,1,0:T(8,128)S(1)} custom-call(bf16[128,96]{1,0:T(8,128)(2,1)S(1)} %get-tuple-element.31.to_uptake, bf16[128,96]{1,0:T(8,128)(2,1)S(1)} %get-tuple-element.32.to_weighted, f32[2,12,4,8,512]{4,3,2,1,0:T(8,128)S(1)} %get-tuple-element.22.both), custom_call_target="tpu_custom_call" | custom-call | tf_op jit(solution)/shard_map/sums/pallas_call | solution.py:264
  10.8 0.9 %inner.1 = f32[12,4,8,512]{3,2,1,0:T(8,128)S(1)} custom-call(f32[12,512]{1,0:T(8,128)S(1)} %get-tuple-element.33.fade, f32[2,12,4,8,512]{4,3,2,1,0:T(8,128)S(1)} %get-tuple-element.22.both, f32[4,8,512]{2,1,0:T(8,128)S(1)} %get-tuple-element.23.vel_u, f32[4,8,512]{2,1,0:T(8,128)S(1)} %get-tuple-element.24.vel_v, f32[4,8,512]{2,1,0:T(8,128)S(1)} %get-tuple-element.25.kappa, ...), custom_call_target="tpu_custom_call" | custom-call | tf_op jit(solution)/shard_map/inner/pallas_call | solution.py:274
  11.7 0.0 collective-permute-done.both
  11.7 1.4 %react.1.inner = f32[12,4,8,512]{3,2,1,0:T(8,128)S(1)} custom-call(bf16[128,96]{1,0:T(8,128)(2,1)S(1)} %get-tuple-element.27.to_uptake, bf16[128,96]{1,0:T(8,128)(2,1)S(1)} %get-tuple-element.28.to_weighted, bf16[192,64]{1,0:T(8,128)(2,1)S(1)} %get-tuple-element.29.to_tracers, f32[4,8,512]{2,1,0:T(8,128)S(1)} %get-tuple-element.30.light, ...), custom_call_target="tpu_custom_call" | custom-call | tf_op jit(solution)/shard_map/react/pallas_call | solution.py:283
  13.1 0.0 collective-permute-done.3.from_fold
  13.1 0.0 collective-permute-done.1.from_west
  13.1 0.0 collective-permute-done.2.from_east
  13.2 1.1 %edges.1 = f32[12,4,8,512]{3,2,1,0:T(8,128)} custom-call(s32[8,128]{1,0:T(8,128)S(1)} %get-tuple-element.21.order, f32[2,12,4,8,512]{4,3,2,1,0:T(8,128)S(1)} %get-tuple-element.22.both, f32[4,8,512]{2,1,0:T(8,128)S(1)} %get-tuple-element.23.vel_u, f32[4,8,512]{2,1,0:T(8,128)S(1)} %get-tuple-element.24.vel_v, f32[4,8,512]{2,1,0:T(8,128)S(1)} %get-tuple-element.25.kappa, ...), custom_call_target="tpu_custom_call" | custom-call | tf_op jit(solution)/shard_map/edges/pallas_call | solution.py:292
Async XLA Ops:
  1.7 10.0 %collective-permute-start = (f32[2,12,4,8,512]{4,3,2,1,0:T(8,128)S(1)}, f32[2,12,4,8,512]{4,3,2,1,0:T(8,128)S(1)}, u32[]{:S(2)}, u32[]{:S(2)}) collective-permute-start(f32[2,12,4,8,512]{4,3,2,1,0:T(8,128)S(1)} %get-tuple-element.22.both), channel_id=1, source_target_pairs={{0,1},{1,0},{2,3},{3,2},{4,5},{5,4},{6,7},{7,6},{8,9},{9,8},{10,11... | collective-permute-start | bytes 4718600 | tf_op jit(solution)/shard_map/ppermute | solution.py:273
  1.8 11.4 %collective-permute-start.1 = (f32[232,128]{1,0:T(8,128)S(1)}, f32[232,128]{1,0:T(8,128)S(1)}, u32[]{:S(2)}, u32[]{:S(2)}) collective-permute-start(f32[232,128]{1,0:T(8,128)S(1)} %get-tuple-element.34), channel_id=1, source_target_pairs={{0,2},{2,4},{4,6},{6,8},{8,10},{10,12},{12,14},{14,0},{1,3},{3,5},... | collective-permute-start | bytes 356360 | tf_op jit(solution)/shard_map/ppermute | solution.py:263
  3.4 9.8 %collective-permute-start.2 = (f32[232,128]{1,0:T(8,128)S(1)}, f32[232,128]{1,0:T(8,128)S(1)}, u32[]{:S(2)}, u32[]{:S(2)}) collective-permute-start(f32[232,128]{1,0:T(8,128)S(1)} %get-tuple-element.35), channel_id=1, source_target_pairs={{0,14},{2,0},{4,2},{6,4},{8,6},{10,8},{12,10},{14,12},{1,15},{3,1}... | collective-permute-start | bytes 356360 | tf_op jit(solution)/shard_map/ppermute | solution.py:262
  3.9 9.3 %collective-permute-start.3 = (f32[8,128]{1,0:T(8,128)S(1)}, f32[8,128]{1,0:T(8,128)S(1)}, u32[]{:S(2)}, u32[]{:S(2)}) collective-permute-start(f32[8,128]{1,0:T(8,128)S(1)} %get-tuple-element.36), channel_id=1, source_target_pairs={{2,12},{4,10},{10,4},{12,2},{3,13},{5,11},{11,5},{13,3},{18,28},{2... | collective-permute-start | bytes 12296 | tf_op jit(solution)/shard_map/ppermute | solution.py:261

commit v4 on v3

--- a/solution.py
+++ b/solution.py
@@ -10,6 +10,10 @@
 SMEM = pl.BlockSpec(memory_space=pltpu.SMEM)
 HBM = pl.BlockSpec(memory_space=pltpu.HBM)
 LANES = 128
+
+
+def is_even():
+    return lax.rem(lax.axis_index("space"), 2) == 0
 
 
 def halves(x):
@@ -43,7 +47,7 @@
 
 def pack_kernel(
     w_in_hbm, w_out_hbm, decay_hbm, partner_hbm, vel_u_hbm, vel_v_hbm, kappa_hbm, sea_hbm, lam_hbm, tracers_hbm, light_hbm,
-    vel_u, vel_v, kappa, sea, light, both, pack_east, pack_west, top_out, to_uptake, to_weighted, to_uptake_other, to_weighted_other, to_tracers, fade, order,
+    vel_u, vel_v, kappa, sea, light, both, pack_even, pack_odd, top_out, to_uptake, to_weighted, to_uptake_other, to_weighted_other, to_tracers, fade, order,
     w_in, w_out, decay, partner, sems,
 ):
     lam, tracers = both.at[0], both.at[1]
@@ -75,7 +79,10 @@
     for copy in copies[4:9]:
         copy.wait()
 
-    for target, line, sign in ((pack_east, slice(cols - 1, cols), -0.5), (pack_west, slice(0, 1), 0.5)):
+    even = is_even()
+    for target, is_east in ((pack_even, even), (pack_odd, jnp.logical_not(even))):
+        line = pl.ds(jnp.where(is_east, cols - 1, 0), 1)
+        sign = jnp.where(is_east, -0.5, 0.5)
 
         def put(index, value):
             for c in range(rows // LANES):
@@ -101,20 +108,11 @@
     for k in range(levels):
         top = placed(top, edge + k, 0.5 * kappa[k, :, last:] - 0.25 * vel_v[k, :, last:])
         top = placed(top, edge + levels + k, sea[k, :, last:].astype(F32))
-    for target in (pack_east, pack_west):
+    for target in (pack_even, pack_odd):
         target[pl.ds(rows // LANES * tall, cols), :] = top
     top_out[...] = top
     for copy in copies[9:]:
         copy.wait()
-
-
-def sums_kernel(to_uptake, to_weighted, both, sums):
-    _, count, levels, cols, rows = both.shape
-    reactions = sums.shape[0] // 2
-    for k in range(levels):
-        for field, matrix, base in ((1, to_uptake, 0), (0, to_weighted, reactions)):
-            total = product(matrix, both[field, :, k].reshape(count * cols, rows))
-            sums[pl.ds(base, reactions), k] = total.reshape(reactions, cols, rows)
 
 
 def inner_kernel(fade, both, vel_u, vel_v, kappa, sea_int, out):
@@ -148,53 +146,74 @@
     lax.fori_loop(0, levels, level, 0)
 
 
-def react_kernel(to_uptake, to_weighted, to_tracers, light, sea, sums, both, inner, out):
+def react_kernel(to_uptake, to_weighted, to_uptake_other, to_weighted_other, to_tracers, light, sea, both, other, inner, out):
     count, levels, cols, rows = inner.shape
-    reactions = sums.shape[0] // 2
+    reactions = to_uptake.shape[0] // (2 * cols)
+
+    def planes(field, k):
+        return field[:, k].reshape(count * cols, rows)
+
     for k in range(levels):
         lit = light[k] * sea[k].astype(F32)
-        uptake = product(to_uptake, both[1, :, k].reshape(count * cols, rows))
-        weighted = product(to_weighted, both[0, :, k].reshape(count * cols, rows))
+        uptake = product(to_uptake, planes(both.at[1], k)) + product(to_uptake_other, planes(other.at[1], k))
+        weighted = product(to_weighted, planes(both.at[0], k)) + product(to_weighted_other, planes(other.at[0], k))
         gain = []
         for h in range(reactions):
             part = slice(h * cols, (h + 1) * cols)
-            t = jnp.tanh(sums[h, k] + uptake[part])
-            gain.append(lit * (1.0 - t * t) * (sums[reactions + h, k] + weighted[part]))
+            t = jnp.tanh(uptake[part])
+            gain.append(lit * (1.0 - t * t) * weighted[part])
         coupled = product(to_tracers, jnp.concatenate(gain, axis=0))
         out[:, k] = inner[:, k] + coupled.reshape(count, cols, rows)
 
 
+def mirrored_by_neighbour():
+    place, strips = lax.axis_index("space"), lax.axis_size("space")
+    neighbour = jnp.where(is_even(), lax.rem(place + strips - 1, strips), lax.rem(place + 1, strips))
+    return neighbour == strips - 1 - place
+
+
+def ordered(order, rows):
+    across = jnp.zeros(rows.shape, F32)
+    for p in range(rows.shape[0]):
+        across = jnp.where(order[...] == p, rows[p : p + 1, :], across)
+    return across
+
+
+def folded_at(across, index):
+    return pltpu.roll(across, LANES - 1 - index, 1)
+
+
+def fold_coef(across, k, edge, levels, vel_v, kappa, sea_int):
+    lane = lax.broadcasted_iota(jnp.int32, across.shape, 1)
+    part = slice(kappa.shape[2] - LANES, kappa.shape[2])
+    up = 0.25 * vel_v[k, :, part] + 0.5 * kappa[k, :, part] + folded_at(across, edge + k)
+    sea = sea_int[k, :, part].astype(F32) * folded_at(across, edge + levels + k)
+    return jnp.where(lane == LANES - 1, sea * up, 0.0)
+
+
 def edges_kernel(
-    order, both, vel_u, vel_v, kappa, sea_int, inner, from_west, from_east, from_fold, out_hbm,
-    out, sems,
+    order, both, vel_u, vel_v, kappa, sea_int, inner, from_even, from_odd, out_hbm, last, out, sems, last_sems
 ):
     lam = both.at[0]
     count, levels, cols, rows = lam.shape
     edge = count * levels
     tall = edge + 2 * levels
     chunks = rows // LANES
-    place, strips = lax.axis_index("space"), lax.axis_size("space")
-    to_east, to_west = lax.rem(place + 1, strips), lax.rem(place + strips - 1, strips)
-    mirror = strips - 1 - place
-    at_fold = pl.ds(chunks * tall, cols)
-    fold_rows = jnp.where(mirror == to_east, from_east[at_fold, :], from_fold[...])
-    fold_rows = jnp.where(mirror == to_west, from_west[at_fold, :], fold_rows)
-    across = jnp.zeros((cols, LANES), F32)
-    for p in range(cols):
-        across = jnp.where(order[...] == p, fold_rows[p : p + 1, :], across)
+    folded = mirrored_by_neighbour()
+    across = ordered(order, jnp.where(folded, from_odd[pl.ds(chunks * tall, cols), :], 0.0))
     sub = lax.broadcasted_iota(jnp.int32, (cols, LANES), 0)
-    lane = lax.broadcasted_iota(jnp.int32, (cols, LANES), 1)
     side = jnp.where(sub == 0, -1.0, jnp.where(sub == cols - 1, 1.0, 0.0))
+    odd_row = jnp.logical_xor(sub == 0, jnp.logical_not(is_even()))
 
     def beyond(c, index):
         at = pl.ds(c * tall + index, 1)
-        return jnp.where(sub == 0, from_west[at, :], from_east[at, :])
-
-    def folded_at(index):
-        return pltpu.roll(across, LANES - 1 - index, 1)
+        return jnp.where(odd_row, from_odd[at, :], from_even[at, :])
 
     def copy(k):
-        return pltpu.make_async_copy(out.at[:, k], out_hbm.at[:, k], sems.at[k])
+        return pltpu.make_async_copy(out.at[:, k], out_hbm.at[:, k, :, pl.ds(0, rows - LANES)], sems.at[k])
+
+    def last_copy(k):
+        return pltpu.make_async_copy(last.at[:, k], out_hbm.at[:, k, :, pl.ds(rows - LANES, LANES)], last_sems.at[k])
 
     def level(k, carry):
         for c in range(chunks):
@@ -203,20 +222,48 @@
             mine = jnp.where(sub == 0, u - kap, u + kap)
             coef = side * sea * beyond(c, edge + levels + k) * (mine + beyond(c, edge + k))
             if c == chunks - 1:
-                up = 0.25 * vel_v[k, :, part] + kap + folded_at(edge + k)
-                fold = jnp.where(lane == LANES - 1, sea * folded_at(edge + levels + k) * up, 0.0)
+                fold = fold_coef(across, k, edge, levels, vel_v, kappa, sea_int)
             for a in range(count):
                 x = lam[a, k, :, part]
                 y = inner[a, k, :, part] + coef * (beyond(c, a * levels + k) - x)
                 if c == chunks - 1:
-                    y += fold * (folded_at(a * levels + k) - x)
-                out[a, k, :, part] = y
+                    last[a, k] = y + fold * (folded_at(across, a * levels + k) - x)
+                else:
+                    out[a, k, :, part] = y
         copy(k).start()
+
+        @pl.when(folded)
+        def _():
+            last_copy(k).start()
+
         return carry
 
     lax.fori_loop(0, levels, level, 0)
     for k in range(levels):
         copy(k).wait()
+
+    @pl.when(folded)
+    def _():
+        for k in range(levels):
+            last_copy(k).wait()
+
+
+def fold_kernel(result, order, both, vel_v, kappa, sea_int, last, from_fold, out_hbm, out, sem):
+    lam = both.at[0]
+    count, levels, cols, rows = lam.shape
+    edge = count * levels
+
+    @pl.when(jnp.logical_not(mirrored_by_neighbour()))
+    def _():
+        across = ordered(order, from_fold[...])
+        for k in range(levels):
+            fold = fold_coef(across, k, edge, levels, vel_v, kappa, sea_int)
+            for a in range(count):
+                x = lam[a, k, :, rows - LANES :]
+                out[a, k] = last[a, k] + fold * (folded_at(across, a * levels + k) - x)
+        copy = pltpu.make_async_copy(out, out_hbm.at[:, :, :, pl.ds(rows - LANES, LANES)], sem)
+        copy.start()
+        copy.wait()
 
 
 def cost(flops, count):
@@ -230,12 +277,11 @@
     n = lax.axis_size("space")
     params = pltpu.CompilerParams(vmem_limit_bytes=32 << 20)
     whole = jax.ShapeDtypeStruct(lam.shape, F32)
-    shares = jax.ShapeDtypeStruct((2 * reactions, levels, cols, rows), F32)
     tile = jax.ShapeDtypeStruct((cols, LANES), F32)
     scalars = (w_in, w_out.T, decay, partner)
     arguments = (vel_u, vel_v, kappa, sea_int, lam, tracers, light)
     whole = jax.ShapeDtypeStruct(lam.shape, F32)
-    vel_u, vel_v, kappa, sea_int, light, both, pack_east, pack_west, top, *spreads, to_tracers, fade, order = pl.pallas_call(
+    vel_u, vel_v, kappa, sea_int, light, both, pack_even, pack_odd, top, *spreads, to_tracers, fade, order = pl.pallas_call(
         pack_kernel,
         name="pack",
         out_shape=(
@@ -255,21 +301,12 @@
         compiler_params=params,
         cost_estimate=cost(0, 4 * lam.size),
     )(*(pltpu.with_memory_space_constraint(x, pltpu.HBM) for x in scalars + arguments))
-    eastward = [(s, (s + 1) % n) for s in range(n)]
-    westward = [(s, (s - 1) % n) for s in range(n)]
+    even_pairs = [(s, s ^ 1) for s in range(n)]
+    odd_pairs = [(s, (s + 1) % n if s % 2 else (s - 1) % n) for s in range(n)]
     mirrored = [(s, n - 1 - s) for s in range(n)]
-    from_fold = lax.ppermute(top, "space", [p for p in mirrored if p not in eastward + westward])
-    from_east = lax.ppermute(pack_west, "space", westward)
-    from_west = lax.ppermute(pack_east, "space", eastward)
-    sums = pl.pallas_call(
-        sums_kernel,
-        name="sums",
-        out_shape=shares,
-        in_specs=[VMEM] * 3,
-        out_specs=VMEM,
-        compiler_params=params,
-        cost_estimate=cost(32 * lam.size, 4 * lam.size),
-    )(*spreads[:2], both)
+    from_fold = lax.ppermute(top, "space", [p for p in mirrored if p not in odd_pairs])
+    from_even = lax.ppermute(pack_even, "space", even_pairs)
+    from_odd = lax.ppermute(pack_odd, "space", odd_pairs)
     both_other = lax.ppermute(both, "tracer", [(0, 1), (1, 0)])
     inner = pl.pallas_call(
         inner_kernel,
@@ -284,24 +321,35 @@
         react_kernel,
         name="react",
         out_shape=whole,
-        in_specs=[VMEM] * 8,
+        in_specs=[VMEM] * 10,
         out_specs=VMEM,
         compiler_params=params,
         cost_estimate=cost(16 * lam.size, 4 * lam.size),
-    )(*spreads[2:], to_tracers, light, sea_int, sums, both_other, inner)
-    return pl.pallas_call(
+    )(*spreads, to_tracers, light, sea_int, both, both_other, inner)
+    lanes = jax.ShapeDtypeStruct((count, levels, cols, LANES), F32)
+    result, last = pl.pallas_call(
         edges_kernel,
         name="edges",
-        out_shape=whole,
-        in_specs=[VMEM] * 10,
-        out_specs=HBM,
+        out_shape=(whole, lanes),
+        in_specs=[VMEM] * 9,
+        out_specs=(HBM, VMEM),
         scratch_shapes=[
-            pltpu.VMEM(lam.shape, F32),
+            pltpu.VMEM((count, levels, cols, rows - LANES), F32),
+            pltpu.SemaphoreType.DMA((levels,)),
             pltpu.SemaphoreType.DMA((levels,)),
         ],
         compiler_params=params,
-        cost_estimate=cost(10 * lam.size, 4 * lam.size),
-    )(order, both, vel_u, vel_v, kappa, sea_int, inner, from_west, from_east, from_fold)
+    )(order, both, vel_u, vel_v, kappa, sea_int, inner, from_even, from_odd)
+    return pl.pallas_call(
+        fold_kernel,
+        name="fold",
+        out_shape=whole,
+        in_specs=[HBM] + [VMEM] * 7,
+        out_specs=HBM,
+        input_output_aliases={0: 0},
+        scratch_shapes=[pltpu.VMEM(lanes.shape, F32), pltpu.SemaphoreType.DMA],
+        compiler_params=params,
+    )(pltpu.with_memory_space_constraint(result, pltpu.HBM), order, both, vel_v, kappa, sea_int, last, from_fold)
 
 
 def solution(mesh):

time: 14.4 us -> 14.1 us (0.979)
  starting transfers between devices: 8.52 us -> 7.51 us
  Pallas kernels: 5.64 us -> 6.26 us
    ppermute x3, starting transfers between devices: 8.45 us -> 7.44 us  [the longest x1 4.34 us: body(): lax.ppermute(top, 'space', [p for p in mirrored if p not in odd_pairs])]
    pallas_call x1, Pallas kernels: 1.39 us -> 1.8 us  [body(): pl.pallas_call(react_kernel, name='react', out_shape=whole, in_specs=[VME...]
    pallas_call x2, Pallas kernels: 1.64 us -> 1.92 us  [the longest x1 1.07 us: body(): pl.pallas_call(edges_kernel, name='edges', out_shape=(whole, lanes), in_s...]
  transfers between devices with their start and end apart: 4 -> 4, of which waited for: 0 -> 0; matrix products, arithmetic and copies ran while one was open for 0% -> 0% of each run, Pallas kernels for 20% -> 27%
where the time goes in v4:
time: 14.1 us; the launch traced here: 13.9 us
  starting transfers between devices  7.51 us (53%)
  Pallas kernels  6.26 us (44%)
    ppermute x1, starting transfers between devices, body(): lax.ppermute(top, 'space', [p for p in mirrored if p not in odd_pairs])  4.34 us
    ppermute x1, starting transfers between devices, body(): from_odd = lax.ppermute(pack_odd, 'space', odd_pairs)  3.03 us
    pallas_call x1, Pallas kernels, body(): pl.pallas_call(react_kernel, name='react', out_shape=whole, in_specs=[VME...  1.8 us
    pallas_call x1, Pallas kernels, body(): pl.pallas_call(pack_kernel, name='pack', out_shape=(*(jax.ShapeDtypeStruc...  1.64 us
    pallas_call x1, Pallas kernels, body(): pl.pallas_call(edges_kernel, name='edges', out_shape=(whole, lanes), in_s...  1.07 us
    pallas_call x1, Pallas kernels, body(): pl.pallas_call(inner_kernel, name='inner', out_shape=whole, in_specs=[VME...  0.9 us
    pallas_call x1, Pallas kernels, body(): pl.pallas_call(fold_kernel, name='fold', out_shape=whole, in_specs=[HBM]...  0.84 us
  transfers between devices with their start and end apart: 4, of which 0 were waited for; matrix products, arithmetic and copies ran while one was open for 0% of the time, Pallas kernels for 27%

profile of v4, /device:TPU:2, one launch (start us, length us, event | category | flops | bytes accessed | tf_op | source)
XLA Modules:
  0.0 13.9 jit_solution(16933237579734146158)
XLA Ops:
  0.0 1.6 %pack.1 = (f32[4,8,512]{2,1,0:T(8,128)S(1)}, f32[4,8,512]{2,1,0:T(8,128)S(1)}, f32[4,8,512]{2,1,0:T(8,128)S(1)}, s32[4,8,512]{2,1,0:T(8,128)S(1)}, f32[4,8,512]{...) custom-call(f32[8,24]{1,0:T(8,128)} %w_in_hbm.1, ...), custom_call_target="tpu_custom_call" | custom-call | tf_op jit(solution)/shard_map/pack/pallas_call | solution.py:284
  1.6 0.1 collective-permute-start
  1.7 0.1 collective-permute-start.1
  1.8 3.0 %collective-permute-start.2 = (f32[232,128]{1,0:T(8,128)S(1)}, f32[232,128]{1,0:T(8,128)S(1)}, u32[]{:S(2)}, u32[]{:S(2)}) collective-permute-start(f32[232,128]{1,0:T(8,128)S(1)} %get-tuple-element.37), channel_id=1, source_target_pairs={{0,14},{2,4},{4,2},{6,8},{8,6},{10,12},{12,10},{14,0},{1,15},{3,5}... | collective-permute-start | bytes 356360 | tf_op jit(solution)/shard_map/ppermute | solution.py:309
  4.8 4.3 %collective-permute-start.3 = (f32[8,128]{1,0:T(8,128)S(1)}, f32[8,128]{1,0:T(8,128)S(1)}, u32[]{:S(2)}, u32[]{:S(2)}) collective-permute-start(f32[8,128]{1,0:T(8,128)S(1)} %get-tuple-element.40), channel_id=1, source_target_pairs={{2,12},{4,10},{10,4},{12,2},{3,13},{5,11},{11,5},{13,3},{18,28},{2... | collective-permute-start | bytes 12296 | tf_op jit(solution)/shard_map/ppermute | solution.py:307
  9.2 0.9 %inner.1 = f32[12,4,8,512]{3,2,1,0:T(8,128)S(1)} custom-call(f32[12,512]{1,0:T(8,128)S(1)} %get-tuple-element.35.fade, f32[2,12,4,8,512]{4,3,2,1,0:T(8,128)S(1)} %get-tuple-element.24.both, f32[4,8,512]{2,1,0:T(8,128)S(1)} %get-tuple-element.25.vel_u, f32[4,8,512]{2,1,0:T(8,128)S(1)} %get-tuple-element.26.vel_v, f32[4,8,512]{2,1,0:T(8,128)S(1)} %get-tuple-element.27.kappa, ...), custom_call_target="tpu_custom_call" | custom-call | tf_op jit(solution)/shard_map/inner/pallas_call | solution.py:311
  10.1 0.0 collective-permute-done.other
  10.1 1.8 %react.1.inner = f32[12,4,8,512]{3,2,1,0:T(8,128)S(1)} custom-call(bf16[128,96]{1,0:T(8,128)(2,1)S(1)} %get-tuple-element.29.to_uptake, bf16[128,96]{1,0:T(8,128)(2,1)S(1)} %get-tuple-element.30.to_weighted, bf16[128,96]{1,0:T(8,128)(2,1)S(1)} %get-tuple-element.31.to_uptake_other, bf16[128,96]{1,0:T(8,128)(2,1)S(1)} %get-tuple-element.32.to_weighted_other, ...), custom_call_target="tpu_custom_call" | custom-call | tf_op jit(solution)/shard_map/react/pallas_call | solution.py:320
  11.9 0.0 collective-permute-done.1.from_even
  11.9 0.0 collective-permute-done.2.from_odd
  11.9 1.1 %edges.1 = (f32[12,4,8,512]{3,2,1,0:T(8,128)}, f32[12,4,8,128]{3,2,1,0:T(8,128)S(1)}) custom-call(s32[8,128]{1,0:T(8,128)S(1)} %get-tuple-element.23.order, f32[2,12,4,8,512]{4,3,2,1,0:T(8,128)S(1)} %get-tuple-element.24.both, f32[4,8,512]{2,1,0:T(8,128)S(1)} %get-tuple-element.25.vel_u, f32[4,8,512]{2,1,0:T(8,128)S(1)} %get-tuple-element.26.vel_v, ...), custom_call_target="tpu_custom_call" | custom-call | tf_op jit(solution)/shard_map/edges/pallas_call | solution.py:330
  13.0 0.0 collective-permute-done.3.from_fold
  13.0 0.8 %fold.1 = f32[12,4,8,512]{3,2,1,0:T(8,128)} custom-call(f32[12,4,8,512]{3,2,1,0:T(8,128)} %get-tuple-element.38.result, s32[8,128]{1,0:T(8,128)S(1)} %get-tuple-element.23.order, f32[2,12,4,8,512]{4,3,2,1,0:T(8,128)S(1)} %get-tuple-element.24.both, f32[4,8,512]{2,1,0:T(8,128)S(1)} %get-tuple-element.26.vel_v, ...), custom_call_target="tpu_custom_call", output_to_operand_aliasing={{}: (0, {})} | custom-call | tf_op jit(solution)/shard_map/fold/pallas_call | solution.py:343
Async XLA Ops:
  1.6 8.4 %collective-permute-start = (f32[2,12,4,8,512]{4,3,2,1,0:T(8,128)S(1)}, f32[2,12,4,8,512]{4,3,2,1,0:T(8,128)S(1)}, u32[]{:S(2)}, u32[]{:S(2)}) collective-permute-start(f32[2,12,4,8,512]{4,3,2,1,0:T(8,128)S(1)} %get-tuple-element.24.both), channel_id=1, source_target_pairs={{0,1},{1,0},{2,3},{3,2},{4,5},{5,4},{6,7},{7,6},{8,9},{9,8},{10,11... | collective-permute-start | bytes 4718600 | tf_op jit(solution)/shard_map/ppermute | solution.py:310
  1.7 10.2 %collective-permute-start.1 = (f32[232,128]{1,0:T(8,128)S(1)}, f32[232,128]{1,0:T(8,128)S(1)}, u32[]{:S(2)}, u32[]{:S(2)}) collective-permute-start(f32[232,128]{1,0:T(8,128)S(1)} %get-tuple-element.36), channel_id=1, source_target_pairs={{0,2},{2,0},{4,6},{6,4},{8,10},{10,8},{12,14},{14,12},{1,3},{3,1},... | collective-permute-start | bytes 356360 | tf_op jit(solution)/shard_map/ppermute | solution.py:308
  1.8 10.1 %collective-permute-start.2 = (f32[232,128]{1,0:T(8,128)S(1)}, f32[232,128]{1,0:T(8,128)S(1)}, u32[]{:S(2)}, u32[]{:S(2)}) collective-permute-start(f32[232,128]{1,0:T(8,128)S(1)} %get-tuple-element.37), channel_id=1, source_target_pairs={{0,14},{2,4},{4,2},{6,8},{8,6},{10,12},{12,10},{14,0},{1,15},{3,5}... | collective-permute-start | bytes 356360 | tf_op jit(solution)/shard_map/ppermute | solution.py:309
  4.8 8.2 %collective-permute-start.3 = (f32[8,128]{1,0:T(8,128)S(1)}, f32[8,128]{1,0:T(8,128)S(1)}, u32[]{:S(2)}, u32[]{:S(2)}) collective-permute-start(f32[8,128]{1,0:T(8,128)S(1)} %get-tuple-element.40), channel_id=1, source_target_pairs={{2,12},{4,10},{10,4},{12,2},{3,13},{5,11},{11,5},{13,3},{18,28},{2... | collective-permute-start | bytes 12296 | tf_op jit(solution)/shard_map/ppermute | solution.py:307

commit v5 on v4

--- a/solution.py
+++ b/solution.py
@@ -21,21 +21,18 @@
     return high, (x - high.astype(F32)).astype(BF16)
 
 
-def spread(target, weight, blocks, width, cols):
-    lane = lax.broadcasted_iota(jnp.int32, (cols, width * cols), 1)
-    sub = lax.broadcasted_iota(jnp.int32, (cols, width * cols), 0)
-    square, diagonal = lane // cols, lane % cols == sub
-    chosen = [square == other for other in range(width)]
-    high, low = [], []
-    for block in range(blocks):
-        row = jnp.zeros((cols, width * cols), F32)
-        for other in range(width):
-            row = jnp.where(chosen[other], weight(block, other), row)
-        row = jnp.where(diagonal, row, 0.0)
-        top = row.astype(BF16).astype(F32)
-        high.append(top)
-        low.append(row - top)
-    target[...] = jnp.concatenate(high + low, axis=0).astype(BF16)
+def spread(target, weights, start, cols):
+    blocks, width = weights.shape[0], target.shape[1]
+    lane = lax.broadcasted_iota(jnp.int32, weights.shape, 1)
+    picked = jnp.take_along_axis(weights, lax.rem(start + lane // cols, LANES), axis=1)
+    diagonal = (lane % cols == lax.broadcasted_iota(jnp.int32, weights.shape, 0))[:cols]
+    rows = [jnp.where(diagonal, jnp.broadcast_to(picked[b : b + 1], (cols, LANES)), 0.0) for b in range(blocks)]
+    whole = jnp.concatenate(rows, axis=0)
+    high, low = halves(whole)
+    half = blocks * cols
+    target[:half] = high[:, :width]
+    target[half:] = low[:, :width]
+    return high, low
 
 
 def product(matrix, x):
@@ -58,8 +55,8 @@
     sources = (w_in_hbm, w_out_hbm, decay_hbm, partner_hbm, vel_u_hbm, vel_v_hbm, kappa_hbm, sea_hbm, lam_hbm, tracers_hbm, light_hbm)
     targets = (w_in, w_out, decay, partner, vel_u, vel_v, kappa, sea, lam, tracers, light)
     copies = [pltpu.make_async_copy(s, t, sems.at[i]) for i, (s, t) in enumerate(zip(sources, targets))]
-    for copy in copies:
-        copy.start()
+    for i in (0, 1, 2, 3, 8, 4, 5, 6, 7, 9, 10):
+        copies[i].start()
     first = lax.axis_index("tracer") * count
     for copy in copies[:4]:
         copy.wait()
@@ -70,12 +67,17 @@
     for i in range(cols):
         picks = jnp.where(sub == i, lax.rem(partner[i], cols), picks)
     order[...] = picks
-    spread(to_uptake, lambda h, a: w_in[h, first + a], reactions, count, cols)
-    spread(to_weighted, lambda h, a: w_out[h, first + a], reactions, count, cols)
     second = count - first
-    spread(to_uptake_other, lambda h, a: w_in[h, second + a], reactions, count, cols)
-    spread(to_weighted_other, lambda h, a: w_out[h, second + a], reactions, count, cols)
-    spread(to_tracers, lambda a, h: w_in[h, first + a], count, reactions, cols)
+    padding = jnp.zeros((reactions, LANES - w_in.shape[1]), F32)
+    inward = jnp.concatenate([w_in[...], padding], axis=1)
+    outward = jnp.concatenate([w_out[...], padding], axis=1)
+    high, low = spread(to_uptake, inward, first, cols)
+    spread(to_weighted, outward, first, cols)
+    spread(to_uptake_other, inward, second, cols)
+    spread(to_weighted_other, outward, second, cols)
+    half = count * cols
+    to_tracers[:half] = high.astype(F32).T[:half].astype(BF16)
+    to_tracers[half:] = low.astype(F32).T[:half].astype(BF16)
     for copy in copies[4:9]:
         copy.wait()
 
@@ -297,7 +299,8 @@
         ),
         in_specs=[HBM] * 11,
         out_specs=(VMEM,) * 16,
-        scratch_shapes=[*(pltpu.SMEM(x.shape, x.dtype) for x in scalars), pltpu.SemaphoreType.DMA((11,))],
+        scratch_shapes=[*(pltpu.VMEM(x.shape, x.dtype) for x in scalars[:2]),
+            *(pltpu.SMEM(x.shape, x.dtype) for x in scalars[2:]), pltpu.SemaphoreType.DMA((11,))],
         compiler_params=params,
         cost_estimate=cost(0, 4 * lam.size),
     )(*(pltpu.with_memory_space_constraint(x, pltpu.HBM) for x in scalars + arguments))

time: 14.1 us -> 14 us (level)
  no operation moved by 1% of the time
where the time goes in v5:
time: 14 us; the launch traced here: 13.8 us
  starting transfers between devices  7.51 us (54%)
  Pallas kernels  6.2 us (44%)
    ppermute x1, starting transfers between devices, body(): lax.ppermute(top, 'space', [p for p in mirrored if p not in odd_pairs])  4.34 us
    ppermute x1, starting transfers between devices, body(): from_odd = lax.ppermute(pack_odd, 'space', odd_pairs)  3.03 us
    pallas_call x1, Pallas kernels, body(): pl.pallas_call(react_kernel, name='react', out_shape=whole, in_specs=[VME...  1.81 us
    pallas_call x1, Pallas kernels, body(): pl.pallas_call(pack_kernel, name='pack', out_shape=(*(jax.ShapeDtypeStruc...  1.58 us
    pallas_call x1, Pallas kernels, body(): pl.pallas_call(edges_kernel, name='edges', out_shape=(whole, lanes), in_s...  1.07 us
    pallas_call x1, Pallas kernels, body(): pl.pallas_call(inner_kernel, name='inner', out_shape=whole, in_specs=[VME...  0.9 us
    pallas_call x1, Pallas kernels, body(): pl.pallas_call(fold_kernel, name='fold', out_shape=whole, in_specs=[HBM]...  0.84 us
  transfers between devices with their start and end apart: 4, of which 0 were waited for; matrix products, arithmetic and copies ran while one was open for 0% of the time, Pallas kernels for 27%

profile of v5, /device:TPU:2, one launch (start us, length us, event | category | flops | bytes accessed | tf_op | source)
XLA Modules:
  0.0 13.8 jit_solution(11177299796864829870)
XLA Ops:
  0.0 1.6 %pack.1 = (f32[4,8,512]{2,1,0:T(8,128)S(1)}, f32[4,8,512]{2,1,0:T(8,128)S(1)}, f32[4,8,512]{2,1,0:T(8,128)S(1)}, s32[4,8,512]{2,1,0:T(8,128)S(1)}, f32[4,8,512]{...) custom-call(f32[8,24]{1,0:T(8,128)} %w_in_hbm.1, ...), custom_call_target="tpu_custom_call" | custom-call | tf_op jit(solution)/shard_map/pack/pallas_call | solution.py:286
  1.6 0.1 collective-permute-start
  1.7 0.1 collective-permute-start.1
  1.7 3.0 %collective-permute-start.2 = (f32[232,128]{1,0:T(8,128)S(1)}, f32[232,128]{1,0:T(8,128)S(1)}, u32[]{:S(2)}, u32[]{:S(2)}) collective-permute-start(f32[232,128]{1,0:T(8,128)S(1)} %get-tuple-element.37), channel_id=1, source_target_pairs={{0,14},{2,4},{4,2},{6,8},{8,6},{10,12},{12,10},{14,0},{1,15},{3,5}... | collective-permute-start | bytes 356360 | tf_op jit(solution)/shard_map/ppermute | solution.py:312
  4.8 4.3 %collective-permute-start.3 = (f32[8,128]{1,0:T(8,128)S(1)}, f32[8,128]{1,0:T(8,128)S(1)}, u32[]{:S(2)}, u32[]{:S(2)}) collective-permute-start(f32[8,128]{1,0:T(8,128)S(1)} %get-tuple-element.40), channel_id=1, source_target_pairs={{2,12},{4,10},{10,4},{12,2},{3,13},{5,11},{11,5},{13,3},{18,28},{2... | collective-permute-start | bytes 12296 | tf_op jit(solution)/shard_map/ppermute | solution.py:310
  9.1 0.9 %inner.1 = f32[12,4,8,512]{3,2,1,0:T(8,128)S(1)} custom-call(f32[12,512]{1,0:T(8,128)S(1)} %get-tuple-element.35.fade, f32[2,12,4,8,512]{4,3,2,1,0:T(8,128)S(1)} %get-tuple-element.24.both, f32[4,8,512]{2,1,0:T(8,128)S(1)} %get-tuple-element.25.vel_u, f32[4,8,512]{2,1,0:T(8,128)S(1)} %get-tuple-element.26.vel_v, f32[4,8,512]{2,1,0:T(8,128)S(1)} %get-tuple-element.27.kappa, ...), custom_call_target="tpu_custom_call" | custom-call | tf_op jit(solution)/shard_map/inner/pallas_call | solution.py:314
  10.0 0.0 collective-permute-done.other
  10.0 1.8 %react.1.inner = f32[12,4,8,512]{3,2,1,0:T(8,128)S(1)} custom-call(bf16[128,96]{1,0:T(8,128)(2,1)S(1)} %get-tuple-element.29.to_uptake, bf16[128,96]{1,0:T(8,128)(2,1)S(1)} %get-tuple-element.30.to_weighted, bf16[128,96]{1,0:T(8,128)(2,1)S(1)} %get-tuple-element.31.to_uptake_other, bf16[128,96]{1,0:T(8,128)(2,1)S(1)} %get-tuple-element.32.to_weighted_other, ...), custom_call_target="tpu_custom_call" | custom-call | tf_op jit(solution)/shard_map/react/pallas_call | solution.py:323
  11.9 0.0 collective-permute-done.1.from_even
  11.9 0.0 collective-permute-done.2.from_odd
  11.9 1.1 %edges.1 = (f32[12,4,8,512]{3,2,1,0:T(8,128)}, f32[12,4,8,128]{3,2,1,0:T(8,128)S(1)}) custom-call(s32[8,128]{1,0:T(8,128)S(1)} %get-tuple-element.23.order, f32[2,12,4,8,512]{4,3,2,1,0:T(8,128)S(1)} %get-tuple-element.24.both, f32[4,8,512]{2,1,0:T(8,128)S(1)} %get-tuple-element.25.vel_u, f32[4,8,512]{2,1,0:T(8,128)S(1)} %get-tuple-element.26.vel_v, ...), custom_call_target="tpu_custom_call" | custom-call | tf_op jit(solution)/shard_map/edges/pallas_call | solution.py:333
  13.0 0.0 collective-permute-done.3.from_fold
  13.0 0.8 %fold.1 = f32[12,4,8,512]{3,2,1,0:T(8,128)} custom-call(f32[12,4,8,512]{3,2,1,0:T(8,128)} %get-tuple-element.38.result, s32[8,128]{1,0:T(8,128)S(1)} %get-tuple-element.23.order, f32[2,12,4,8,512]{4,3,2,1,0:T(8,128)S(1)} %get-tuple-element.24.both, f32[4,8,512]{2,1,0:T(8,128)S(1)} %get-tuple-element.26.vel_v, ...), custom_call_target="tpu_custom_call", output_to_operand_aliasing={{}: (0, {})} | custom-call | tf_op jit(solution)/shard_map/fold/pallas_call | solution.py:346
Async XLA Ops:
  1.6 8.4 %collective-permute-start = (f32[2,12,4,8,512]{4,3,2,1,0:T(8,128)S(1)}, f32[2,12,4,8,512]{4,3,2,1,0:T(8,128)S(1)}, u32[]{:S(2)}, u32[]{:S(2)}) collective-permute-start(f32[2,12,4,8,512]{4,3,2,1,0:T(8,128)S(1)} %get-tuple-element.24.both), channel_id=1, source_target_pairs={{0,1},{1,0},{2,3},{3,2},{4,5},{5,4},{6,7},{7,6},{8,9},{9,8},{10,11... | collective-permute-start | bytes 4718600 | tf_op jit(solution)/shard_map/ppermute | solution.py:313
  1.7 10.2 %collective-permute-start.1 = (f32[232,128]{1,0:T(8,128)S(1)}, f32[232,128]{1,0:T(8,128)S(1)}, u32[]{:S(2)}, u32[]{:S(2)}) collective-permute-start(f32[232,128]{1,0:T(8,128)S(1)} %get-tuple-element.36), channel_id=1, source_target_pairs={{0,2},{2,0},{4,6},{6,4},{8,10},{10,8},{12,14},{14,12},{1,3},{3,1},... | collective-permute-start | bytes 356360 | tf_op jit(solution)/shard_map/ppermute | solution.py:311
  1.7 10.1 %collective-permute-start.2 = (f32[232,128]{1,0:T(8,128)S(1)}, f32[232,128]{1,0:T(8,128)S(1)}, u32[]{:S(2)}, u32[]{:S(2)}) collective-permute-start(f32[232,128]{1,0:T(8,128)S(1)} %get-tuple-element.37), channel_id=1, source_target_pairs={{0,14},{2,4},{4,2},{6,8},{8,6},{10,12},{12,10},{14,0},{1,15},{3,5}... | collective-permute-start | bytes 356360 | tf_op jit(solution)/shard_map/ppermute | solution.py:312
  4.8 8.2 %collective-permute-start.3 = (f32[8,128]{1,0:T(8,128)S(1)}, f32[8,128]{1,0:T(8,128)S(1)}, u32[]{:S(2)}, u32[]{:S(2)}) collective-permute-start(f32[8,128]{1,0:T(8,128)S(1)} %get-tuple-element.40), channel_id=1, source_target_pairs={{2,12},{4,10},{10,4},{12,2},{3,13},{5,11},{11,5},{13,3},{18,28},{2... | collective-permute-start | bytes 12296 | tf_op jit(solution)/shard_map/ppermute | solution.py:310
